TPU v7x, 512 devices: a whole 4x8x8 slice. The times are simulated.
512 devices in a mesh: tm: 16 (over x, y_lo, core), slab: 32 (over y_hi, z).
Axes of the slice: x: 4, y: 8 (y_hi: 4, y_lo: 2; y = y_hi * 2 + y_lo), z: 8, core: 2. Of those that a mesh axis runs over, the one named last changes fastest.
Arguments:
- slice_starts: float32 [16, 2, 128, 16, 512], P('tm', None, 'slab'), may hold values from 0 to 1
- class_map: int32 [128, 16, 512], P('slab'), may hold values from 0 to 3
- table: float32 [4, 2], replicated, may hold values from 0.03 to 0.16
Outputs:
- final_states: float32 [16, 2, 128, 16, 512], P('tm', None, 'slab')
All inputs are finite; a program needn't handle non-finite values.
Results may differ from a plain program's by a relative error of at most 0.000071.
Values sent between devices are 32-bit elements; how exact they have to be, the bound alone decides.
A program may use at most 64 MiB of HBM per device.

v0:
```python
import jax
import jax.numpy as jnp
from jax import lax
from jax.sharding import PartitionSpec as P

FINE = 4
ITERS = 2
CLASSES = 4


FEED = 0.04
KILL = 0.062
STEP = 0.04


def with_halo(cells, sides, width):
    for axis, dim in sides:
        count = lax.axis_size(axis)
        head = lax.slice_in_dim(cells, 0, width, axis=dim)
        tail = lax.slice_in_dim(cells, cells.shape[dim] - width, cells.shape[dim], axis=dim)
        cells = jnp.concatenate(
            [
                lax.ppermute(tail, axis, [(i, (i + 1) % count) for i in range(count)]),
                cells,
                lax.ppermute(head, axis, [((i + 1) % count, i) for i in range(count)]),
            ],
            axis=dim,
        )
    return cells


def from_behind(block, axis, distance):
    devices = range(lax.axis_size(axis))
    route = [(i - distance, i) for i in devices if i - distance in devices]
    return lax.ppermute(block, axis, route)


def reaction(field):
    u_part = field[0]
    v_part = field[1]
    uvv = u_part * v_part * v_part
    return jnp.stack([-uvv + FEED * (1.0 - u_part), uvv - (FEED + KILL) * v_part])


def inplane(field):
    return (
        jnp.roll(field, 1, -1)
        + jnp.roll(field, -1, -1)
        + jnp.roll(field, 1, -2)
        + jnp.roll(field, -1, -2)
    )


def coefficients(class_map, table):
    lam = jnp.zeros((2,) + class_map.shape, jnp.float32)
    for klass in range(CLASSES):
        lam = lam + jnp.where(
            class_map[None] == klass, table[klass][:, None, None, None], jnp.float32(0.0)
        )
    return lam


def fine_update(padded, lam_core):
    core = padded[:, 1:-1]
    lap = padded[:, 2:] + padded[:, :-2] + inplane(core) - 6.0 * core
    return core + lam_core * lap + STEP * reaction(core)


def coarse_prop(field, coarse_lam):
    return field + coarse_lam * (inplane(field) - 4.0 * field) + FINE * STEP * reaction(field)


def on_device(slice_starts, class_map, table):
    exact = slice_starts[0]
    state = exact
    lam = coefficients(class_map, table)
    coarse_lam = FINE * lam / (1.0 + 4.0 * FINE * lam)
    index = lax.axis_index("tm")
    first = index == 0
    n_time = lax.axis_size("tm")
    ends = state
    for sweep in range(ITERS):
        field = state
        for step in range(FINE):
            padded = with_halo(field, (("slab", 1),), 1)
            field = fine_update(padded, lam)
        corr = field - coarse_prop(state, coarse_lam)

        def relay(count, current):
            result = coarse_prop(current, coarse_lam) + corr
            arrived = from_behind(result, "tm", 1)
            return jnp.where(first, exact, arrived)

        state = lax.fori_loop(0, n_time - 1, relay, state)
        ends = coarse_prop(state, coarse_lam) + corr
    return ends[None]


def solution(mesh):
    in_specs = (P("tm", None, "slab", None, None), P("slab", None, None), P())
    out_specs = P("tm", None, "slab", None, None)
    return jax.shard_map(
        on_device, mesh=mesh, in_specs=in_specs, out_specs=out_specs, check_vma=False
    )
```

profile of v0, /device:TPU:7, one launch (start us, length us, event | category | flops | bytes accessed | tf_op | source)
XLA Modules:
  0.0 397.2 jit_solution(5218057417146322771)
XLA Ops:
  0.9 14.4 %collective-permute-start.2 = (f32[2,1,16,512]{3,2,1,0:T(8,128)S(1)}, f32[2,1,16,512]{3,2,1,0:T(8,128)S(1)}, u32[]{:S(2)}, u32[]{:S(2)}) collective-permute-start(f32[2,1,16,512]{3,2,1,0:T(8,128)S(1)} %get-tuple-element.327), channel_id=1, source_target_pairs={{1,0},{2,1},{3,2},{4,3},{5,4},{6,5},{7,6},{8,7},{9,8},{10,9},{11,1... | collective-permute-start | bytes 196616 | tf_op jit(solution)/shard_map/ppermute | solution.py:25
  19.5 5.4 %collective-permute-done.3 = f32[2,1,16,512]{3,2,1,0:T(8,128)S(1)} collective-permute-done((f32[2,1,16,512]{3,2,1,0:T(8,128)S(1)}, f32[2,1,16,512]{3,2,1,0:T(8,128)S(1)}, u32[]{:S(2)}, u32[]{:S(2)}) %collective-permute-start.3) | collective-permute-done | bytes 65568 | tf_op jit(solution)/shard_map/ppermute | solution.py:23
  30.8 6.8 %collective-permute-done.5 = f32[2,1,16,512]{3,2,1,0:T(8,128)S(1)} collective-permute-done((f32[2,1,16,512]{3,2,1,0:T(8,128)S(1)}, f32[2,1,16,512]{3,2,1,0:T(8,128)S(1)}, u32[]{:S(2)}, u32[]{:S(2)}) %collective-permute-start.5) | collective-permute-done | bytes 65568 | tf_op jit(solution)/shard_map/ppermute | solution.py:23
  40.3 3.4 collective-permute-start.7
  43.7 6.3 %collective-permute-done.7 = f32[2,1,16,512]{3,2,1,0:T(8,128)S(1)} collective-permute-done((f32[2,1,16,512]{3,2,1,0:T(8,128)S(1)}, f32[2,1,16,512]{3,2,1,0:T(8,128)S(1)}, u32[]{:S(2)}, u32[]{:S(2)}) %collective-permute-start.7) | collective-permute-done | bytes 65568 | tf_op jit(solution)/shard_map/ppermute | solution.py:23
  52.5 3.4 collective-permute-start.9
  56.0 5.8 %collective-permute-done.9 = f32[2,1,16,512]{3,2,1,0:T(8,128)S(1)} collective-permute-done((f32[2,1,16,512]{3,2,1,0:T(8,128)S(1)}, f32[2,1,16,512]{3,2,1,0:T(8,128)S(1)}, u32[]{:S(2)}, u32[]{:S(2)}) %collective-permute-start.9) | collective-permute-done | bytes 65568 | tf_op jit(solution)/shard_map/ppermute | solution.py:23
  62.2 138.8 %while.22 = (s32[]{:T(128)}, f32[2,4,16,512]{3,2,1,0:T(8,128)S(1)}, pred[]{:T(512)}, f32[2,4,16,512]{3,2,1,0:T(8,128)S(1)}, f32[2,4,16,512]{3,2,1,0:T(8,128)S(1)...) while((s32[]{:T(128)}, f32[2,4,16,512]{3,2,1,0:T(8,128)S(1)}, ...), condition=%wide.region_1.2_spmd.clone, body=%wide.region_0.1_spmd.clone.sunk | while | flops 2031618 | bytes 6684878 | solution.py:94
  63.0 6.5 %collective-permute-start = (f32[2,4,16,512]{3,2,1,0:T(8,128)S(1)}, f32[2,4,16,512]{3,2,1,0:T(8,128)S(1)}, u32[]{:S(2)}, u32[]{:S(2)}) collective-permute-start(f32[2,4,16,512]{3,2,1,0:T(8,128)S(1)} %fusion.163), channel_id=1, source_target_pairs={{0,32},{32,64},{64,96},{96,128},{128,160},{160,192},{192,224},{224... | collective-permute-start | bytes 786440 | tf_op jit(solution)/shard_map/while/body/eval_jaxpr/ppermute | solution.py:35
  73.5 4.4 %collective-permute-start = (f32[2,4,16,512]{3,2,1,0:T(8,128)S(1)}, f32[2,4,16,512]{3,2,1,0:T(8,128)S(1)}, u32[]{:S(2)}, u32[]{:S(2)}) collective-permute-start(f32[2,4,16,512]{3,2,1,0:T(8,128)S(1)} %fusion.163), channel_id=1, source_target_pairs={{0,32},{32,64},{64,96},{96,128},{128,160},{160,192},{192,224},{224... | collective-permute-start | bytes 786440 | tf_op jit(solution)/shard_map/while/body/eval_jaxpr/ppermute | solution.py:35
  81.9 4.4 %collective-permute-start = (f32[2,4,16,512]{3,2,1,0:T(8,128)S(1)}, f32[2,4,16,512]{3,2,1,0:T(8,128)S(1)}, u32[]{:S(2)}, u32[]{:S(2)}) collective-permute-start(f32[2,4,16,512]{3,2,1,0:T(8,128)S(1)} %fusion.163), channel_id=1, source_target_pairs={{0,32},{32,64},{64,96},{96,128},{128,160},{160,192},{192,224},{224... | collective-permute-start | bytes 786440 | tf_op jit(solution)/shard_map/while/body/eval_jaxpr/ppermute | solution.py:35
  90.4 4.4 %collective-permute-start = (f32[2,4,16,512]{3,2,1,0:T(8,128)S(1)}, f32[2,4,16,512]{3,2,1,0:T(8,128)S(1)}, u32[]{:S(2)}, u32[]{:S(2)}) collective-permute-start(f32[2,4,16,512]{3,2,1,0:T(8,128)S(1)} %fusion.163), channel_id=1, source_target_pairs={{0,32},{32,64},{64,96},{96,128},{128,160},{160,192},{192,224},{224... | collective-permute-start | bytes 786440 | tf_op jit(solution)/shard_map/while/body/eval_jaxpr/ppermute | solution.py:35
  98.9 4.4 %collective-permute-start = (f32[2,4,16,512]{3,2,1,0:T(8,128)S(1)}, f32[2,4,16,512]{3,2,1,0:T(8,128)S(1)}, u32[]{:S(2)}, u32[]{:S(2)}) collective-permute-start(f32[2,4,16,512]{3,2,1,0:T(8,128)S(1)} %fusion.163), channel_id=1, source_target_pairs={{0,32},{32,64},{64,96},{96,128},{128,160},{160,192},{192,224},{224... | collective-permute-start | bytes 786440 | tf_op jit(solution)/shard_map/while/body/eval_jaxpr/ppermute | solution.py:35
  103.3 4.2 %collective-permute-done = f32[2,4,16,512]{3,2,1,0:T(8,128)S(1)} collective-permute-done((f32[2,4,16,512]{3,2,1,0:T(8,128)S(1)}, f32[2,4,16,512]{3,2,1,0:T(8,128)S(1)}, u32[]{:S(2)}, u32[]{:S(2)}) %collective-permute-start) | collective-permute-done | bytes 262176 | tf_op jit(solution)/shard_map/while/body/eval_jaxpr/ppermute | solution.py:35
  108.2 3.5 collective-permute-start
  111.7 5.1 %collective-permute-done = f32[2,4,16,512]{3,2,1,0:T(8,128)S(1)} collective-permute-done((f32[2,4,16,512]{3,2,1,0:T(8,128)S(1)}, f32[2,4,16,512]{3,2,1,0:T(8,128)S(1)}, u32[]{:S(2)}, u32[]{:S(2)}) %collective-permute-start) | collective-permute-done | bytes 262176 | tf_op jit(solution)/shard_map/while/body/eval_jaxpr/ppermute | solution.py:35
  120.2 6.0 %collective-permute-done = f32[2,4,16,512]{3,2,1,0:T(8,128)S(1)} collective-permute-done((f32[2,4,16,512]{3,2,1,0:T(8,128)S(1)}, f32[2,4,16,512]{3,2,1,0:T(8,128)S(1)}, u32[]{:S(2)}, u32[]{:S(2)}) %collective-permute-start) | collective-permute-done | bytes 262176 | tf_op jit(solution)/shard_map/while/body/eval_jaxpr/ppermute | solution.py:35
  128.9 6.7 %collective-permute-done = f32[2,4,16,512]{3,2,1,0:T(8,128)S(1)} collective-permute-done((f32[2,4,16,512]{3,2,1,0:T(8,128)S(1)}, f32[2,4,16,512]{3,2,1,0:T(8,128)S(1)}, u32[]{:S(2)}, u32[]{:S(2)}) %collective-permute-start) | collective-permute-done | bytes 262176 | tf_op jit(solution)/shard_map/while/body/eval_jaxpr/ppermute | solution.py:35
  138.2 6.7 %collective-permute-done = f32[2,4,16,512]{3,2,1,0:T(8,128)S(1)} collective-permute-done((f32[2,4,16,512]{3,2,1,0:T(8,128)S(1)}, f32[2,4,16,512]{3,2,1,0:T(8,128)S(1)}, u32[]{:S(2)}, u32[]{:S(2)}) %collective-permute-start) | collective-permute-done | bytes 262176 | tf_op jit(solution)/shard_map/while/body/eval_jaxpr/ppermute | solution.py:35
  147.6 6.7 %collective-permute-done = f32[2,4,16,512]{3,2,1,0:T(8,128)S(1)} collective-permute-done((f32[2,4,16,512]{3,2,1,0:T(8,128)S(1)}, f32[2,4,16,512]{3,2,1,0:T(8,128)S(1)}, u32[]{:S(2)}, u32[]{:S(2)}) %collective-permute-start) | collective-permute-done | bytes 262176 | tf_op jit(solution)/shard_map/while/body/eval_jaxpr/ppermute | solution.py:35
  156.9 6.7 %collective-permute-done = f32[2,4,16,512]{3,2,1,0:T(8,128)S(1)} collective-permute-done((f32[2,4,16,512]{3,2,1,0:T(8,128)S(1)}, f32[2,4,16,512]{3,2,1,0:T(8,128)S(1)}, u32[]{:S(2)}, u32[]{:S(2)}) %collective-permute-start) | collective-permute-done | bytes 262176 | tf_op jit(solution)/shard_map/while/body/eval_jaxpr/ppermute | solution.py:35
  166.3 6.7 %collective-permute-done = f32[2,4,16,512]{3,2,1,0:T(8,128)S(1)} collective-permute-done((f32[2,4,16,512]{3,2,1,0:T(8,128)S(1)}, f32[2,4,16,512]{3,2,1,0:T(8,128)S(1)}, u32[]{:S(2)}, u32[]{:S(2)}) %collective-permute-start) | collective-permute-done | bytes 262176 | tf_op jit(solution)/shard_map/while/body/eval_jaxpr/ppermute | solution.py:35
  175.6 6.7 %collective-permute-done = f32[2,4,16,512]{3,2,1,0:T(8,128)S(1)} collective-permute-done((f32[2,4,16,512]{3,2,1,0:T(8,128)S(1)}, f32[2,4,16,512]{3,2,1,0:T(8,128)S(1)}, u32[]{:S(2)}, u32[]{:S(2)}) %collective-permute-start) | collective-permute-done | bytes 262176 | tf_op jit(solution)/shard_map/while/body/eval_jaxpr/ppermute | solution.py:35
  185.0 6.7 %collective-permute-done = f32[2,4,16,512]{3,2,1,0:T(8,128)S(1)} collective-permute-done((f32[2,4,16,512]{3,2,1,0:T(8,128)S(1)}, f32[2,4,16,512]{3,2,1,0:T(8,128)S(1)}, u32[]{:S(2)}, u32[]{:S(2)}) %collective-permute-start) | collective-permute-done | bytes 262176 | tf_op jit(solution)/shard_map/while/body/eval_jaxpr/ppermute | solution.py:35
  194.4 6.7 %collective-permute-done = f32[2,4,16,512]{3,2,1,0:T(8,128)S(1)} collective-permute-done((f32[2,4,16,512]{3,2,1,0:T(8,128)S(1)}, f32[2,4,16,512]{3,2,1,0:T(8,128)S(1)}, u32[]{:S(2)}, u32[]{:S(2)}) %collective-permute-start) | collective-permute-done | bytes 262176 | tf_op jit(solution)/shard_map/while/body/eval_jaxpr/ppermute | solution.py:35
  203.3 3.4 collective-permute-start.11
  206.7 6.0 %collective-permute-done.11 = f32[2,1,16,512]{3,2,1,0:T(8,128)S(1)} collective-permute-done((f32[2,1,16,512]{3,2,1,0:T(8,128)S(1)}, f32[2,1,16,512]{3,2,1,0:T(8,128)S(1)}, u32[]{:S(2)}, u32[]{:S(2)}) %collective-permute-start.11) | collective-permute-done | bytes 65568 | tf_op jit(solution)/shard_map/ppermute | solution.py:23
  215.3 3.4 collective-permute-start.13
  218.7 5.9 %collective-permute-done.13 = f32[2,1,16,512]{3,2,1,0:T(8,128)S(1)} collective-permute-done((f32[2,1,16,512]{3,2,1,0:T(8,128)S(1)}, f32[2,1,16,512]{3,2,1,0:T(8,128)S(1)}, u32[]{:S(2)}, u32[]{:S(2)}) %collective-permute-start.13) | collective-permute-done | bytes 65568 | tf_op jit(solution)/shard_map/ppermute | solution.py:23
  230.7 5.8 %collective-permute-done.15 = f32[2,1,16,512]{3,2,1,0:T(8,128)S(1)} collective-permute-done((f32[2,1,16,512]{3,2,1,0:T(8,128)S(1)}, f32[2,1,16,512]{3,2,1,0:T(8,128)S(1)}, u32[]{:S(2)}, u32[]{:S(2)}) %collective-permute-start.15) | collective-permute-done | bytes 65568 | tf_op jit(solution)/shard_map/ppermute | solution.py:23
  242.5 5.8 %collective-permute-done.17 = f32[2,1,16,512]{3,2,1,0:T(8,128)S(1)} collective-permute-done((f32[2,1,16,512]{3,2,1,0:T(8,128)S(1)}, f32[2,1,16,512]{3,2,1,0:T(8,128)S(1)}, u32[]{:S(2)}, u32[]{:S(2)}) %collective-permute-start.17) | collective-permute-done | bytes 65568 | tf_op jit(solution)/shard_map/ppermute | solution.py:23
  248.8 147.0 %while.23 = (s32[]{:T(128)}, f32[2,4,16,512]{3,2,1,0:T(8,128)S(1)}, pred[]{:T(512)}, f32[2,4,16,512]{3,2,1,0:T(8,128)S(1)}, f32[2,4,16,512]{3,2,1,0:T(8,128)S(1)...) while((s32[]{:T(128)}, f32[2,4,16,512]{3,2,1,0:T(8,128)S(1)}, ...), condition=%wide.region_3.4_spmd.clone, body=%wide.region_2.3_spmd.clone.sunk | while | flops 2031618 | bytes 6684878 | solution.py:94
  249.5 6.0 %collective-permute-start.1 = (f32[2,4,16,512]{3,2,1,0:T(8,128)S(1)}, f32[2,4,16,512]{3,2,1,0:T(8,128)S(1)}, u32[]{:S(2)}, u32[]{:S(2)}) collective-permute-start(f32[2,4,16,512]{3,2,1,0:T(8,128)S(1)} %fusion.168), channel_id=1, source_target_pairs={{0,32},{32,64},{64,96},{96,128},{128,160},{160,192},{192,224},{224... | collective-permute-start | bytes 786440 | tf_op jit(solution)/shard_map/while/body/eval_jaxpr/ppermute | solution.py:35
  255.6 9.2 %collective-permute-done.1 = f32[2,4,16,512]{3,2,1,0:T(8,128)S(1)} collective-permute-done((f32[2,4,16,512]{3,2,1,0:T(8,128)S(1)}, f32[2,4,16,512]{3,2,1,0:T(8,128)S(1)}, u32[]{:S(2)}, u32[]{:S(2)}) %collective-permute-start.1) | collective-permute-done | bytes 262176 | tf_op jit(solution)/shard_map/while/body/eval_jaxpr/ppermute | solution.py:35
  267.4 6.7 %collective-permute-done.1 = f32[2,4,16,512]{3,2,1,0:T(8,128)S(1)} collective-permute-done((f32[2,4,16,512]{3,2,1,0:T(8,128)S(1)}, f32[2,4,16,512]{3,2,1,0:T(8,128)S(1)}, u32[]{:S(2)}, u32[]{:S(2)}) %collective-permute-start.1) | collective-permute-done | bytes 262176 | tf_op jit(solution)/shard_map/while/body/eval_jaxpr/ppermute | solution.py:35
  276.8 6.7 %collective-permute-done.1 = f32[2,4,16,512]{3,2,1,0:T(8,128)S(1)} collective-permute-done((f32[2,4,16,512]{3,2,1,0:T(8,128)S(1)}, f32[2,4,16,512]{3,2,1,0:T(8,128)S(1)}, u32[]{:S(2)}, u32[]{:S(2)}) %collective-permute-start.1) | collective-permute-done | bytes 262176 | tf_op jit(solution)/shard_map/while/body/eval_jaxpr/ppermute | solution.py:35
  286.2 6.7 %collective-permute-done.1 = f32[2,4,16,512]{3,2,1,0:T(8,128)S(1)} collective-permute-done((f32[2,4,16,512]{3,2,1,0:T(8,128)S(1)}, f32[2,4,16,512]{3,2,1,0:T(8,128)S(1)}, u32[]{:S(2)}, u32[]{:S(2)}) %collective-permute-start.1) | collective-permute-done | bytes 262176 | tf_op jit(solution)/shard_map/while/body/eval_jaxpr/ppermute | solution.py:35
  295.5 6.7 %collective-permute-done.1 = f32[2,4,16,512]{3,2,1,0:T(8,128)S(1)} collective-permute-done((f32[2,4,16,512]{3,2,1,0:T(8,128)S(1)}, f32[2,4,16,512]{3,2,1,0:T(8,128)S(1)}, u32[]{:S(2)}, u32[]{:S(2)}) %collective-permute-start.1) | collective-permute-done | bytes 262176 | tf_op jit(solution)/shard_map/while/body/eval_jaxpr/ppermute | solution.py:35
  304.9 6.7 %collective-permute-done.1 = f32[2,4,16,512]{3,2,1,0:T(8,128)S(1)} collective-permute-done((f32[2,4,16,512]{3,2,1,0:T(8,128)S(1)}, f32[2,4,16,512]{3,2,1,0:T(8,128)S(1)}, u32[]{:S(2)}, u32[]{:S(2)}) %collective-permute-start.1) | collective-permute-done | bytes 262176 | tf_op jit(solution)/shard_map/while/body/eval_jaxpr/ppermute | solution.py:35
  314.2 6.7 %collective-permute-done.1 = f32[2,4,16,512]{3,2,1,0:T(8,128)S(1)} collective-permute-done((f32[2,4,16,512]{3,2,1,0:T(8,128)S(1)}, f32[2,4,16,512]{3,2,1,0:T(8,128)S(1)}, u32[]{:S(2)}, u32[]{:S(2)}) %collective-permute-start.1) | collective-permute-done | bytes 262176 | tf_op jit(solution)/shard_map/while/body/eval_jaxpr/ppermute | solution.py:35
  323.6 6.7 %collective-permute-done.1 = f32[2,4,16,512]{3,2,1,0:T(8,128)S(1)} collective-permute-done((f32[2,4,16,512]{3,2,1,0:T(8,128)S(1)}, f32[2,4,16,512]{3,2,1,0:T(8,128)S(1)}, u32[]{:S(2)}, u32[]{:S(2)}) %collective-permute-start.1) | collective-permute-done | bytes 262176 | tf_op jit(solution)/shard_map/while/body/eval_jaxpr/ppermute | solution.py:35
  332.9 6.7 %collective-permute-done.1 = f32[2,4,16,512]{3,2,1,0:T(8,128)S(1)} collective-permute-done((f32[2,4,16,512]{3,2,1,0:T(8,128)S(1)}, f32[2,4,16,512]{3,2,1,0:T(8,128)S(1)}, u32[]{:S(2)}, u32[]{:S(2)}) %collective-permute-start.1) | collective-permute-done | bytes 262176 | tf_op jit(solution)/shard_map/while/body/eval_jaxpr/ppermute | solution.py:35
  342.3 6.7 %collective-permute-done.1 = f32[2,4,16,512]{3,2,1,0:T(8,128)S(1)} collective-permute-done((f32[2,4,16,512]{3,2,1,0:T(8,128)S(1)}, f32[2,4,16,512]{3,2,1,0:T(8,128)S(1)}, u32[]{:S(2)}, u32[]{:S(2)}) %collective-permute-start.1) | collective-permute-done | bytes 262176 | tf_op jit(solution)/shard_map/while/body/eval_jaxpr/ppermute | solution.py:35
  351.7 6.7 %collective-permute-done.1 = f32[2,4,16,512]{3,2,1,0:T(8,128)S(1)} collective-permute-done((f32[2,4,16,512]{3,2,1,0:T(8,128)S(1)}, f32[2,4,16,512]{3,2,1,0:T(8,128)S(1)}, u32[]{:S(2)}, u32[]{:S(2)}) %collective-permute-start.1) | collective-permute-done | bytes 262176 | tf_op jit(solution)/shard_map/while/body/eval_jaxpr/ppermute | solution.py:35
  361.0 6.7 %collective-permute-done.1 = f32[2,4,16,512]{3,2,1,0:T(8,128)S(1)} collective-permute-done((f32[2,4,16,512]{3,2,1,0:T(8,128)S(1)}, f32[2,4,16,512]{3,2,1,0:T(8,128)S(1)}, u32[]{:S(2)}, u32[]{:S(2)}) %collective-permute-start.1) | collective-permute-done | bytes 262176 | tf_op jit(solution)/shard_map/while/body/eval_jaxpr/ppermute | solution.py:35
  370.4 6.7 %collective-permute-done.1 = f32[2,4,16,512]{3,2,1,0:T(8,128)S(1)} collective-permute-done((f32[2,4,16,512]{3,2,1,0:T(8,128)S(1)}, f32[2,4,16,512]{3,2,1,0:T(8,128)S(1)}, u32[]{:S(2)}, u32[]{:S(2)}) %collective-permute-start.1) | collective-permute-done | bytes 262176 | tf_op jit(solution)/shard_map/while/body/eval_jaxpr/ppermute | solution.py:35
  379.7 6.7 %collective-permute-done.1 = f32[2,4,16,512]{3,2,1,0:T(8,128)S(1)} collective-permute-done((f32[2,4,16,512]{3,2,1,0:T(8,128)S(1)}, f32[2,4,16,512]{3,2,1,0:T(8,128)S(1)}, u32[]{:S(2)}, u32[]{:S(2)}) %collective-permute-start.1) | collective-permute-done | bytes 262176 | tf_op jit(solution)/shard_map/while/body/eval_jaxpr/ppermute | solution.py:35
  389.1 6.7 %collective-permute-done.1 = f32[2,4,16,512]{3,2,1,0:T(8,128)S(1)} collective-permute-done((f32[2,4,16,512]{3,2,1,0:T(8,128)S(1)}, f32[2,4,16,512]{3,2,1,0:T(8,128)S(1)}, u32[]{:S(2)}, u32[]{:S(2)}) %collective-permute-start.1) | collective-permute-done | bytes 262176 | tf_op jit(solution)/shard_map/while/body/eval_jaxpr/ppermute | solution.py:35
  (327 shorter events, 114.7 us)
Async XLA Ops:
  0.0 17.2 %copy-start = (f32[1,2,4,16,512]{4,3,2,1,0:T(8,128)S(1)}, f32[1,2,4,16,512]{4,3,2,1,0:T(8,128)}, u32[]{:S(2)}) copy-start(f32[1,2,4,16,512]{4,3,2,1,0:T(8,128)} %param.7) | copy-start | bytes 786436
  0.9 18.5 %collective-permute-start.2 = (f32[2,1,16,512]{3,2,1,0:T(8,128)S(1)}, f32[2,1,16,512]{3,2,1,0:T(8,128)S(1)}, u32[]{:S(2)}, u32[]{:S(2)}) collective-permute-start(f32[2,1,16,512]{3,2,1,0:T(8,128)S(1)} %get-tuple-element.327), channel_id=1, source_target_pairs={{1,0},{2,1},{3,2},{4,3},{5,4},{6,5},{7,6},{8,7},{9,8},{10,9},{11,1... | collective-permute-start | bytes 196616 | tf_op jit(solution)/shard_map/ppermute | solution.py:25
  15.3 9.5 %collective-permute-start.3 = (f32[2,1,16,512]{3,2,1,0:T(8,128)S(1)}, f32[2,1,16,512]{3,2,1,0:T(8,128)S(1)}, u32[]{:S(2)}, u32[]{:S(2)}) collective-permute-start(f32[2,1,16,512]{3,2,1,0:T(8,128)S(1)} %get-tuple-element.328), channel_id=1, source_target_pairs={{0,1},{1,2},{2,3},{3,4},{4,5},{5,6},{6,7},{7,8},{8,9},{9,10},{10,1... | collective-permute-start | bytes 196616 | tf_op jit(solution)/shard_map/ppermute | solution.py:23
  17.6 0.9 copy-start.1
  25.5 5.3 %collective-permute-start.4 = (f32[2,1,16,512]{3,2,1,0:T(8,128)S(1)}, f32[2,1,16,512]{3,2,1,0:T(8,128)S(1)}, u32[]{:S(2)}, u32[]{:S(2)}) collective-permute-start(f32[2,1,16,512]{3,2,1,0:T(8,128)S(1)} %get-tuple-element.315), channel_id=1, source_target_pairs={{1,0},{2,1},{3,2},{4,3},{5,4},{6,5},{7,6},{8,7},{9,8},{10,9},{11,1... | collective-permute-start | bytes 196616 | tf_op jit(solution)/shard_map/ppermute | solution.py:25
  27.7 9.9 %collective-permute-start.5 = (f32[2,1,16,512]{3,2,1,0:T(8,128)S(1)}, f32[2,1,16,512]{3,2,1,0:T(8,128)S(1)}, u32[]{:S(2)}, u32[]{:S(2)}) collective-permute-start(f32[2,1,16,512]{3,2,1,0:T(8,128)S(1)} %get-tuple-element.316), channel_id=1, source_target_pairs={{0,1},{1,2},{2,3},{3,4},{4,5},{5,6},{6,7},{7,8},{8,9},{9,10},{10,1... | collective-permute-start | bytes 196616 | tf_op jit(solution)/shard_map/ppermute | solution.py:23
  38.4 5.3 %collective-permute-start.6 = (f32[2,1,16,512]{3,2,1,0:T(8,128)S(1)}, f32[2,1,16,512]{3,2,1,0:T(8,128)S(1)}, u32[]{:S(2)}, u32[]{:S(2)}) collective-permute-start(f32[2,1,16,512]{3,2,1,0:T(8,128)S(1)} %get-tuple-element.303), channel_id=1, source_target_pairs={{1,0},{2,1},{3,2},{4,3},{5,4},{6,5},{7,6},{8,7},{9,8},{10,9},{11,1... | collective-permute-start | bytes 196616 | tf_op jit(solution)/shard_map/ppermute | solution.py:25
  40.3 9.7 %collective-permute-start.7 = (f32[2,1,16,512]{3,2,1,0:T(8,128)S(1)}, f32[2,1,16,512]{3,2,1,0:T(8,128)S(1)}, u32[]{:S(2)}, u32[]{:S(2)}) collective-permute-start(f32[2,1,16,512]{3,2,1,0:T(8,128)S(1)} %get-tuple-element.304), channel_id=1, source_target_pairs={{0,1},{1,2},{2,3},{3,4},{4,5},{5,6},{6,7},{7,8},{8,9},{9,10},{10,1... | collective-permute-start | bytes 196616 | tf_op jit(solution)/shard_map/ppermute | solution.py:23
  50.6 5.3 %collective-permute-start.8 = (f32[2,1,16,512]{3,2,1,0:T(8,128)S(1)}, f32[2,1,16,512]{3,2,1,0:T(8,128)S(1)}, u32[]{:S(2)}, u32[]{:S(2)}) collective-permute-start(f32[2,1,16,512]{3,2,1,0:T(8,128)S(1)} %get-tuple-element.291), channel_id=1, source_target_pairs={{1,0},{2,1},{3,2},{4,3},{5,4},{6,5},{7,6},{8,7},{9,8},{10,9},{11,1... | collective-permute-start | bytes 196616 | tf_op jit(solution)/shard_map/ppermute | solution.py:25
  52.5 9.2 %collective-permute-start.9 = (f32[2,1,16,512]{3,2,1,0:T(8,128)S(1)}, f32[2,1,16,512]{3,2,1,0:T(8,128)S(1)}, u32[]{:S(2)}, u32[]{:S(2)}) collective-permute-start(f32[2,1,16,512]{3,2,1,0:T(8,128)S(1)} %get-tuple-element.292), channel_id=1, source_target_pairs={{0,1},{1,2},{2,3},{3,4},{4,5},{5,6},{6,7},{7,8},{8,9},{9,10},{10,1... | collective-permute-start | bytes 196616 | tf_op jit(solution)/shard_map/ppermute | solution.py:23
  63.0 9.8 %collective-permute-start = (f32[2,4,16,512]{3,2,1,0:T(8,128)S(1)}, f32[2,4,16,512]{3,2,1,0:T(8,128)S(1)}, u32[]{:S(2)}, u32[]{:S(2)}) collective-permute-start(f32[2,4,16,512]{3,2,1,0:T(8,128)S(1)} %fusion.163), channel_id=1, source_target_pairs={{0,32},{32,64},{64,96},{96,128},{128,160},{160,192},{192,224},{224... | collective-permute-start | bytes 786440 | tf_op jit(solution)/shard_map/while/body/eval_jaxpr/ppermute | solution.py:35
  73.5 7.7 %collective-permute-start = (f32[2,4,16,512]{3,2,1,0:T(8,128)S(1)}, f32[2,4,16,512]{3,2,1,0:T(8,128)S(1)}, u32[]{:S(2)}, u32[]{:S(2)}) collective-permute-start(f32[2,4,16,512]{3,2,1,0:T(8,128)S(1)} %fusion.163), channel_id=1, source_target_pairs={{0,32},{32,64},{64,96},{96,128},{128,160},{160,192},{192,224},{224... | collective-permute-start | bytes 786440 | tf_op jit(solution)/shard_map/while/body/eval_jaxpr/ppermute | solution.py:35
  81.9 7.7 %collective-permute-start = (f32[2,4,16,512]{3,2,1,0:T(8,128)S(1)}, f32[2,4,16,512]{3,2,1,0:T(8,128)S(1)}, u32[]{:S(2)}, u32[]{:S(2)}) collective-permute-start(f32[2,4,16,512]{3,2,1,0:T(8,128)S(1)} %fusion.163), channel_id=1, source_target_pairs={{0,32},{32,64},{64,96},{96,128},{128,160},{160,192},{192,224},{224... | collective-permute-start | bytes 786440 | tf_op jit(solution)/shard_map/while/body/eval_jaxpr/ppermute | solution.py:35
  90.4 7.7 %collective-permute-start = (f32[2,4,16,512]{3,2,1,0:T(8,128)S(1)}, f32[2,4,16,512]{3,2,1,0:T(8,128)S(1)}, u32[]{:S(2)}, u32[]{:S(2)}) collective-permute-start(f32[2,4,16,512]{3,2,1,0:T(8,128)S(1)} %fusion.163), channel_id=1, source_target_pairs={{0,32},{32,64},{64,96},{96,128},{128,160},{160,192},{192,224},{224... | collective-permute-start | bytes 786440 | tf_op jit(solution)/shard_map/while/body/eval_jaxpr/ppermute | solution.py:35
  98.9 8.6 %collective-permute-start = (f32[2,4,16,512]{3,2,1,0:T(8,128)S(1)}, f32[2,4,16,512]{3,2,1,0:T(8,128)S(1)}, u32[]{:S(2)}, u32[]{:S(2)}) collective-permute-start(f32[2,4,16,512]{3,2,1,0:T(8,128)S(1)} %fusion.163), channel_id=1, source_target_pairs={{0,32},{32,64},{64,96},{96,128},{128,160},{160,192},{192,224},{224... | collective-permute-start | bytes 786440 | tf_op jit(solution)/shard_map/while/body/eval_jaxpr/ppermute | solution.py:35
  108.2 8.6 %collective-permute-start = (f32[2,4,16,512]{3,2,1,0:T(8,128)S(1)}, f32[2,4,16,512]{3,2,1,0:T(8,128)S(1)}, u32[]{:S(2)}, u32[]{:S(2)}) collective-permute-start(f32[2,4,16,512]{3,2,1,0:T(8,128)S(1)} %fusion.163), channel_id=1, source_target_pairs={{0,32},{32,64},{64,96},{96,128},{128,160},{160,192},{192,224},{224... | collective-permute-start | bytes 786440 | tf_op jit(solution)/shard_map/while/body/eval_jaxpr/ppermute | solution.py:35
  117.6 8.6 %collective-permute-start = (f32[2,4,16,512]{3,2,1,0:T(8,128)S(1)}, f32[2,4,16,512]{3,2,1,0:T(8,128)S(1)}, u32[]{:S(2)}, u32[]{:S(2)}) collective-permute-start(f32[2,4,16,512]{3,2,1,0:T(8,128)S(1)} %fusion.163), channel_id=1, source_target_pairs={{0,32},{32,64},{64,96},{96,128},{128,160},{160,192},{192,224},{224... | collective-permute-start | bytes 786440 | tf_op jit(solution)/shard_map/while/body/eval_jaxpr/ppermute | solution.py:35
  126.9 8.6 %collective-permute-start = (f32[2,4,16,512]{3,2,1,0:T(8,128)S(1)}, f32[2,4,16,512]{3,2,1,0:T(8,128)S(1)}, u32[]{:S(2)}, u32[]{:S(2)}) collective-permute-start(f32[2,4,16,512]{3,2,1,0:T(8,128)S(1)} %fusion.163), channel_id=1, source_target_pairs={{0,32},{32,64},{64,96},{96,128},{128,160},{160,192},{192,224},{224... | collective-permute-start | bytes 786440 | tf_op jit(solution)/shard_map/while/body/eval_jaxpr/ppermute | solution.py:35
  136.3 8.6 %collective-permute-start = (f32[2,4,16,512]{3,2,1,0:T(8,128)S(1)}, f32[2,4,16,512]{3,2,1,0:T(8,128)S(1)}, u32[]{:S(2)}, u32[]{:S(2)}) collective-permute-start(f32[2,4,16,512]{3,2,1,0:T(8,128)S(1)} %fusion.163), channel_id=1, source_target_pairs={{0,32},{32,64},{64,96},{96,128},{128,160},{160,192},{192,224},{224... | collective-permute-start | bytes 786440 | tf_op jit(solution)/shard_map/while/body/eval_jaxpr/ppermute | solution.py:35
  145.6 8.6 %collective-permute-start = (f32[2,4,16,512]{3,2,1,0:T(8,128)S(1)}, f32[2,4,16,512]{3,2,1,0:T(8,128)S(1)}, u32[]{:S(2)}, u32[]{:S(2)}) collective-permute-start(f32[2,4,16,512]{3,2,1,0:T(8,128)S(1)} %fusion.163), channel_id=1, source_target_pairs={{0,32},{32,64},{64,96},{96,128},{128,160},{160,192},{192,224},{224... | collective-permute-start | bytes 786440 | tf_op jit(solution)/shard_map/while/body/eval_jaxpr/ppermute | solution.py:35
  155.0 8.6 %collective-permute-start = (f32[2,4,16,512]{3,2,1,0:T(8,128)S(1)}, f32[2,4,16,512]{3,2,1,0:T(8,128)S(1)}, u32[]{:S(2)}, u32[]{:S(2)}) collective-permute-start(f32[2,4,16,512]{3,2,1,0:T(8,128)S(1)} %fusion.163), channel_id=1, source_target_pairs={{0,32},{32,64},{64,96},{96,128},{128,160},{160,192},{192,224},{224... | collective-permute-start | bytes 786440 | tf_op jit(solution)/shard_map/while/body/eval_jaxpr/ppermute | solution.py:35
  164.4 8.6 %collective-permute-start = (f32[2,4,16,512]{3,2,1,0:T(8,128)S(1)}, f32[2,4,16,512]{3,2,1,0:T(8,128)S(1)}, u32[]{:S(2)}, u32[]{:S(2)}) collective-permute-start(f32[2,4,16,512]{3,2,1,0:T(8,128)S(1)} %fusion.163), channel_id=1, source_target_pairs={{0,32},{32,64},{64,96},{96,128},{128,160},{160,192},{192,224},{224... | collective-permute-start | bytes 786440 | tf_op jit(solution)/shard_map/while/body/eval_jaxpr/ppermute | solution.py:35
  173.7 8.6 %collective-permute-start = (f32[2,4,16,512]{3,2,1,0:T(8,128)S(1)}, f32[2,4,16,512]{3,2,1,0:T(8,128)S(1)}, u32[]{:S(2)}, u32[]{:S(2)}) collective-permute-start(f32[2,4,16,512]{3,2,1,0:T(8,128)S(1)} %fusion.163), channel_id=1, source_target_pairs={{0,32},{32,64},{64,96},{96,128},{128,160},{160,192},{192,224},{224... | collective-permute-start | bytes 786440 | tf_op jit(solution)/shard_map/while/body/eval_jaxpr/ppermute | solution.py:35
  183.1 8.6 %collective-permute-start = (f32[2,4,16,512]{3,2,1,0:T(8,128)S(1)}, f32[2,4,16,512]{3,2,1,0:T(8,128)S(1)}, u32[]{:S(2)}, u32[]{:S(2)}) collective-permute-start(f32[2,4,16,512]{3,2,1,0:T(8,128)S(1)} %fusion.163), channel_id=1, source_target_pairs={{0,32},{32,64},{64,96},{96,128},{128,160},{160,192},{192,224},{224... | collective-permute-start | bytes 786440 | tf_op jit(solution)/shard_map/while/body/eval_jaxpr/ppermute | solution.py:35
  192.4 8.6 %collective-permute-start = (f32[2,4,16,512]{3,2,1,0:T(8,128)S(1)}, f32[2,4,16,512]{3,2,1,0:T(8,128)S(1)}, u32[]{:S(2)}, u32[]{:S(2)}) collective-permute-start(f32[2,4,16,512]{3,2,1,0:T(8,128)S(1)} %fusion.163), channel_id=1, source_target_pairs={{0,32},{32,64},{64,96},{96,128},{128,160},{160,192},{192,224},{224... | collective-permute-start | bytes 786440 | tf_op jit(solution)/shard_map/while/body/eval_jaxpr/ppermute | solution.py:35
  201.4 5.3 %collective-permute-start.10 = (f32[2,1,16,512]{3,2,1,0:T(8,128)S(1)}, f32[2,1,16,512]{3,2,1,0:T(8,128)S(1)}, u32[]{:S(2)}, u32[]{:S(2)}) collective-permute-start(f32[2,1,16,512]{3,2,1,0:T(8,128)S(1)} %get-tuple-element.279), channel_id=1, source_target_pairs={{1,0},{2,1},{3,2},{4,3},{5,4},{6,5},{7,6},{8,7},{9,8},{10,9},{11,1... | collective-permute-start | bytes 196616 | tf_op jit(solution)/shard_map/ppermute | solution.py:25
  203.3 9.4 %collective-permute-start.11 = (f32[2,1,16,512]{3,2,1,0:T(8,128)S(1)}, f32[2,1,16,512]{3,2,1,0:T(8,128)S(1)}, u32[]{:S(2)}, u32[]{:S(2)}) collective-permute-start(f32[2,1,16,512]{3,2,1,0:T(8,128)S(1)} %get-tuple-element.280), channel_id=1, source_target_pairs={{0,1},{1,2},{2,3},{3,4},{4,5},{5,6},{6,7},{7,8},{8,9},{9,10},{10,1... | collective-permute-start | bytes 196616 | tf_op jit(solution)/shard_map/ppermute | solution.py:23
  213.4 5.3 %collective-permute-start.12 = (f32[2,1,16,512]{3,2,1,0:T(8,128)S(1)}, f32[2,1,16,512]{3,2,1,0:T(8,128)S(1)}, u32[]{:S(2)}, u32[]{:S(2)}) collective-permute-start(f32[2,1,16,512]{3,2,1,0:T(8,128)S(1)} %get-tuple-element.267), channel_id=1, source_target_pairs={{1,0},{2,1},{3,2},{4,3},{5,4},{6,5},{7,6},{8,7},{9,8},{10,9},{11,1... | collective-permute-start | bytes 196616 | tf_op jit(solution)/shard_map/ppermute | solution.py:25
  215.3 9.3 %collective-permute-start.13 = (f32[2,1,16,512]{3,2,1,0:T(8,128)S(1)}, f32[2,1,16,512]{3,2,1,0:T(8,128)S(1)}, u32[]{:S(2)}, u32[]{:S(2)}) collective-permute-start(f32[2,1,16,512]{3,2,1,0:T(8,128)S(1)} %get-tuple-element.268), channel_id=1, source_target_pairs={{0,1},{1,2},{2,3},{3,4},{4,5},{5,6},{6,7},{7,8},{8,9},{9,10},{10,1... | collective-permute-start | bytes 196616 | tf_op jit(solution)/shard_map/ppermute | solution.py:23
  225.3 5.3 %collective-permute-start.14 = (f32[2,1,16,512]{3,2,1,0:T(8,128)S(1)}, f32[2,1,16,512]{3,2,1,0:T(8,128)S(1)}, u32[]{:S(2)}, u32[]{:S(2)}) collective-permute-start(f32[2,1,16,512]{3,2,1,0:T(8,128)S(1)} %get-tuple-element.255), channel_id=1, source_target_pairs={{1,0},{2,1},{3,2},{4,3},{5,4},{6,5},{7,6},{8,7},{9,8},{10,9},{11,1... | collective-permute-start | bytes 196616 | tf_op jit(solution)/shard_map/ppermute | solution.py:25
  227.3 9.2 %collective-permute-start.15 = (f32[2,1,16,512]{3,2,1,0:T(8,128)S(1)}, f32[2,1,16,512]{3,2,1,0:T(8,128)S(1)}, u32[]{:S(2)}, u32[]{:S(2)}) collective-permute-start(f32[2,1,16,512]{3,2,1,0:T(8,128)S(1)} %get-tuple-element.256), channel_id=1, source_target_pairs={{0,1},{1,2},{2,3},{3,4},{4,5},{5,6},{6,7},{7,8},{8,9},{9,10},{10,1... | collective-permute-start | bytes 196616 | tf_op jit(solution)/shard_map/ppermute | solution.py:23
  237.2 5.3 %collective-permute-start.16 = (f32[2,1,16,512]{3,2,1,0:T(8,128)S(1)}, f32[2,1,16,512]{3,2,1,0:T(8,128)S(1)}, u32[]{:S(2)}, u32[]{:S(2)}) collective-permute-start(f32[2,1,16,512]{3,2,1,0:T(8,128)S(1)} %get-tuple-element.243), channel_id=1, source_target_pairs={{1,0},{2,1},{3,2},{4,3},{5,4},{6,5},{7,6},{8,7},{9,8},{10,9},{11,1... | collective-permute-start | bytes 196616 | tf_op jit(solution)/shard_map/ppermute | solution.py:25
  239.1 9.2 %collective-permute-start.17 = (f32[2,1,16,512]{3,2,1,0:T(8,128)S(1)}, f32[2,1,16,512]{3,2,1,0:T(8,128)S(1)}, u32[]{:S(2)}, u32[]{:S(2)}) collective-permute-start(f32[2,1,16,512]{3,2,1,0:T(8,128)S(1)} %get-tuple-element.244), channel_id=1, source_target_pairs={{0,1},{1,2},{2,3},{3,4},{4,5},{5,6},{6,7},{7,8},{8,9},{9,10},{10,1... | collective-permute-start | bytes 196616 | tf_op jit(solution)/shard_map/ppermute | solution.py:23
  249.5 15.2 %collective-permute-start.1 = (f32[2,4,16,512]{3,2,1,0:T(8,128)S(1)}, f32[2,4,16,512]{3,2,1,0:T(8,128)S(1)}, u32[]{:S(2)}, u32[]{:S(2)}) collective-permute-start(f32[2,4,16,512]{3,2,1,0:T(8,128)S(1)} %fusion.168), channel_id=1, source_target_pairs={{0,32},{32,64},{64,96},{96,128},{128,160},{160,192},{192,224},{224... | collective-permute-start | bytes 786440 | tf_op jit(solution)/shard_map/while/body/eval_jaxpr/ppermute | solution.py:35
  265.5 8.6 %collective-permute-start.1 = (f32[2,4,16,512]{3,2,1,0:T(8,128)S(1)}, f32[2,4,16,512]{3,2,1,0:T(8,128)S(1)}, u32[]{:S(2)}, u32[]{:S(2)}) collective-permute-start(f32[2,4,16,512]{3,2,1,0:T(8,128)S(1)} %fusion.168), channel_id=1, source_target_pairs={{0,32},{32,64},{64,96},{96,128},{128,160},{160,192},{192,224},{224... | collective-permute-start | bytes 786440 | tf_op jit(solution)/shard_map/while/body/eval_jaxpr/ppermute | solution.py:35
  274.9 8.6 %collective-permute-start.1 = (f32[2,4,16,512]{3,2,1,0:T(8,128)S(1)}, f32[2,4,16,512]{3,2,1,0:T(8,128)S(1)}, u32[]{:S(2)}, u32[]{:S(2)}) collective-permute-start(f32[2,4,16,512]{3,2,1,0:T(8,128)S(1)} %fusion.168), channel_id=1, source_target_pairs={{0,32},{32,64},{64,96},{96,128},{128,160},{160,192},{192,224},{224... | collective-permute-start | bytes 786440 | tf_op jit(solution)/shard_map/while/body/eval_jaxpr/ppermute | solution.py:35
  284.2 8.6 %collective-permute-start.1 = (f32[2,4,16,512]{3,2,1,0:T(8,128)S(1)}, f32[2,4,16,512]{3,2,1,0:T(8,128)S(1)}, u32[]{:S(2)}, u32[]{:S(2)}) collective-permute-start(f32[2,4,16,512]{3,2,1,0:T(8,128)S(1)} %fusion.168), channel_id=1, source_target_pairs={{0,32},{32,64},{64,96},{96,128},{128,160},{160,192},{192,224},{224... | collective-permute-start | bytes 786440 | tf_op jit(solution)/shard_map/while/body/eval_jaxpr/ppermute | solution.py:35
  293.6 8.6 %collective-permute-start.1 = (f32[2,4,16,512]{3,2,1,0:T(8,128)S(1)}, f32[2,4,16,512]{3,2,1,0:T(8,128)S(1)}, u32[]{:S(2)}, u32[]{:S(2)}) collective-permute-start(f32[2,4,16,512]{3,2,1,0:T(8,128)S(1)} %fusion.168), channel_id=1, source_target_pairs={{0,32},{32,64},{64,96},{96,128},{128,160},{160,192},{192,224},{224... | collective-permute-start | bytes 786440 | tf_op jit(solution)/shard_map/while/body/eval_jaxpr/ppermute | solution.py:35
  302.9 8.6 %collective-permute-start.1 = (f32[2,4,16,512]{3,2,1,0:T(8,128)S(1)}, f32[2,4,16,512]{3,2,1,0:T(8,128)S(1)}, u32[]{:S(2)}, u32[]{:S(2)}) collective-permute-start(f32[2,4,16,512]{3,2,1,0:T(8,128)S(1)} %fusion.168), channel_id=1, source_target_pairs={{0,32},{32,64},{64,96},{96,128},{128,160},{160,192},{192,224},{224... | collective-permute-start | bytes 786440 | tf_op jit(solution)/shard_map/while/body/eval_jaxpr/ppermute | solution.py:35
  312.3 8.6 %collective-permute-start.1 = (f32[2,4,16,512]{3,2,1,0:T(8,128)S(1)}, f32[2,4,16,512]{3,2,1,0:T(8,128)S(1)}, u32[]{:S(2)}, u32[]{:S(2)}) collective-permute-start(f32[2,4,16,512]{3,2,1,0:T(8,128)S(1)} %fusion.168), channel_id=1, source_target_pairs={{0,32},{32,64},{64,96},{96,128},{128,160},{160,192},{192,224},{224... | collective-permute-start | bytes 786440 | tf_op jit(solution)/shard_map/while/body/eval_jaxpr/ppermute | solution.py:35
  321.7 8.6 %collective-permute-start.1 = (f32[2,4,16,512]{3,2,1,0:T(8,128)S(1)}, f32[2,4,16,512]{3,2,1,0:T(8,128)S(1)}, u32[]{:S(2)}, u32[]{:S(2)}) collective-permute-start(f32[2,4,16,512]{3,2,1,0:T(8,128)S(1)} %fusion.168), channel_id=1, source_target_pairs={{0,32},{32,64},{64,96},{96,128},{128,160},{160,192},{192,224},{224... | collective-permute-start | bytes 786440 | tf_op jit(solution)/shard_map/while/body/eval_jaxpr/ppermute | solution.py:35
  331.0 8.6 %collective-permute-start.1 = (f32[2,4,16,512]{3,2,1,0:T(8,128)S(1)}, f32[2,4,16,512]{3,2,1,0:T(8,128)S(1)}, u32[]{:S(2)}, u32[]{:S(2)}) collective-permute-start(f32[2,4,16,512]{3,2,1,0:T(8,128)S(1)} %fusion.168), channel_id=1, source_target_pairs={{0,32},{32,64},{64,96},{96,128},{128,160},{160,192},{192,224},{224... | collective-permute-start | bytes 786440 | tf_op jit(solution)/shard_map/while/body/eval_jaxpr/ppermute | solution.py:35
  340.4 8.6 %collective-permute-start.1 = (f32[2,4,16,512]{3,2,1,0:T(8,128)S(1)}, f32[2,4,16,512]{3,2,1,0:T(8,128)S(1)}, u32[]{:S(2)}, u32[]{:S(2)}) collective-permute-start(f32[2,4,16,512]{3,2,1,0:T(8,128)S(1)} %fusion.168), channel_id=1, source_target_pairs={{0,32},{32,64},{64,96},{96,128},{128,160},{160,192},{192,224},{224... | collective-permute-start | bytes 786440 | tf_op jit(solution)/shard_map/while/body/eval_jaxpr/ppermute | solution.py:35
  349.7 8.6 %collective-permute-start.1 = (f32[2,4,16,512]{3,2,1,0:T(8,128)S(1)}, f32[2,4,16,512]{3,2,1,0:T(8,128)S(1)}, u32[]{:S(2)}, u32[]{:S(2)}) collective-permute-start(f32[2,4,16,512]{3,2,1,0:T(8,128)S(1)} %fusion.168), channel_id=1, source_target_pairs={{0,32},{32,64},{64,96},{96,128},{128,160},{160,192},{192,224},{224... | collective-permute-start | bytes 786440 | tf_op jit(solution)/shard_map/while/body/eval_jaxpr/ppermute | solution.py:35
  359.1 8.6 %collective-permute-start.1 = (f32[2,4,16,512]{3,2,1,0:T(8,128)S(1)}, f32[2,4,16,512]{3,2,1,0:T(8,128)S(1)}, u32[]{:S(2)}, u32[]{:S(2)}) collective-permute-start(f32[2,4,16,512]{3,2,1,0:T(8,128)S(1)} %fusion.168), channel_id=1, source_target_pairs={{0,32},{32,64},{64,96},{96,128},{128,160},{160,192},{192,224},{224... | collective-permute-start | bytes 786440 | tf_op jit(solution)/shard_map/while/body/eval_jaxpr/ppermute | solution.py:35
  368.4 8.6 %collective-permute-start.1 = (f32[2,4,16,512]{3,2,1,0:T(8,128)S(1)}, f32[2,4,16,512]{3,2,1,0:T(8,128)S(1)}, u32[]{:S(2)}, u32[]{:S(2)}) collective-permute-start(f32[2,4,16,512]{3,2,1,0:T(8,128)S(1)} %fusion.168), channel_id=1, source_target_pairs={{0,32},{32,64},{64,96},{96,128},{128,160},{160,192},{192,224},{224... | collective-permute-start | bytes 786440 | tf_op jit(solution)/shard_map/while/body/eval_jaxpr/ppermute | solution.py:35
  377.8 8.6 %collective-permute-start.1 = (f32[2,4,16,512]{3,2,1,0:T(8,128)S(1)}, f32[2,4,16,512]{3,2,1,0:T(8,128)S(1)}, u32[]{:S(2)}, u32[]{:S(2)}) collective-permute-start(f32[2,4,16,512]{3,2,1,0:T(8,128)S(1)} %fusion.168), channel_id=1, source_target_pairs={{0,32},{32,64},{64,96},{96,128},{128,160},{160,192},{192,224},{224... | collective-permute-start | bytes 786440 | tf_op jit(solution)/shard_map/while/body/eval_jaxpr/ppermute | solution.py:35
  387.2 8.6 %collective-permute-start.1 = (f32[2,4,16,512]{3,2,1,0:T(8,128)S(1)}, f32[2,4,16,512]{3,2,1,0:T(8,128)S(1)}, u32[]{:S(2)}, u32[]{:S(2)}) collective-permute-start(f32[2,4,16,512]{3,2,1,0:T(8,128)S(1)} %fusion.168), channel_id=1, source_target_pairs={{0,32},{32,64},{64,96},{96,128},{128,160},{160,192},{192,224},{224... | collective-permute-start | bytes 786440 | tf_op jit(solution)/shard_map/while/body/eval_jaxpr/ppermute | solution.py:35
  (1 other events, 0.7 us)
where the time goes:
time: 404 us; the launch traced here: 397 us
  waiting for transfers between devices  232 us (57%)
  starting transfers between devices  132 us (33%)
  other arithmetic  17.3 us (4%)
  local copies, waits for them, and re-layouts  14 us (3%)
    ppermute x30, waiting for transfers between devices, from_behind(): return lax.ppermute(block, axis, route)  184 us
    ppermute x30, starting transfers between devices, from_behind(): return lax.ppermute(block, axis, route)  78.4 us
    ppermute x8, waiting for transfers between devices, with_halo(): lax.ppermute(tail, axis, [(i, (i + 1) % count) for i in range(count)])  47.8 us
    ppermute x8, starting transfers between devices, with_halo(): lax.ppermute(head, axis, [((i + 1) % count, i) for i in range(count)])  28.1 us
    ppermute x8, starting transfers between devices, with_halo(): lax.ppermute(tail, axis, [(i, (i + 1) % count) for i in range(count)])  25.1 us
    add x30, other arithmetic, relay(): result = coarse_prop(current, coarse_lam) + corr  10.6 us
  transfers between devices with their start and end apart: 46, of which 38 were waited for; matrix products, arithmetic and copies ran while one was open for 0% of the time, Pallas kernels for 0%

commit v1 on v0

v1 whole, which is shorter than its diff:
```python
import functools

import jax
import jax.numpy as jnp
from jax import lax
from jax.experimental import pallas as pl
from jax.experimental.pallas import tpu as pltpu
from jax.sharding import PartitionSpec as P

FINE = 4
CLASSES = 4
NTS = 16
FEED = 0.04
KILL = 0.062
STEP = 0.04
PLANES = 4
ROWS = 16
COLS = 512
LANES = 128
CHUNKS = COLS // LANES
HALO = FINE
DEEP = PLANES + 2 * HALO
PIECE = 2 * ROWS + 8
MESH = pl.DeviceIdType.MESH


def react(u, v, scale):
    uvv = u * v * v
    return scale * (FEED * (1.0 - u) - uvv), scale * (uvv - (FEED + KILL) * v)


def four(a):
    rows, cols = a.shape
    return (
        pltpu.roll(a, 1, 1)
        + pltpu.roll(a, cols - 1, 1)
        + pltpu.roll(a, 1, 0)
        + pltpu.roll(a, rows - 1, 0)
    )


def coarse(u, v, cu, cv):
    ru, rv = react(u, v, FINE * STEP)
    return u + cu * (four(u) - 4.0 * u) + ru, v + cv * (four(v) - 4.0 * v) + rv


def coarse_of(lam):
    return FINE * lam / (1.0 + 4.0 * FINE * lam)


def kernel(
    ss, cm_in, table, out,
    lv, cm, lam, gb, pack, got, made,
    load_sem, hs, hr, cs, cr, ps, pr, vs, vr,
):
    t = lax.axis_index("tm")
    s = lax.axis_index("slab")
    slabs = lax.axis_size("slab")
    up = lax.rem(s + 1, slabs)
    down = lax.rem(s + slabs - 1, slabs)
    my_plane = t // CHUNKS
    my_chunk = lax.rem(t, CHUNKS)

    def at_slab(z):
        return (t, z)

    barrier = pltpu.get_barrier_semaphore()
    for z in (up, down):
        pl.semaphore_signal(barrier, inc=1, device_id=at_slab(z), device_id_type=MESH)

    def greet(k, carry):
        peer = lax.rem(t + k, NTS)
        pl.semaphore_signal(barrier, inc=1, device_id=(peer, s), device_id_type=MESH)
        return carry

    lax.fori_loop(1, NTS, greet, 0)

    loads = [
        pltpu.make_async_copy(ss.at[0, :, p], lv.at[0, HALO + p], load_sem.at[p])
        for p in range(PLANES)
    ]
    loads.append(pltpu.make_async_copy(cm_in, cm.at[pl.ds(HALO, PLANES)], load_sem.at[PLANES]))
    for copy in loads:
        copy.start()
    pl.semaphore_wait(barrier, NTS + 1)

    def halo_copies(sweep, i):
        if sweep == 0:
            tail, head = ss.at[0, :, PLANES - 1 - i], ss.at[0, :, i]
        else:
            tail, head = lv.at[4, HALO + PLANES - 1 - i], lv.at[4, HALO + i]
        return [
            pltpu.make_async_remote_copy(
                src_ref=src,
                dst_ref=lv.at[4 * sweep, plane],
                send_sem=hs.at[sweep, way, i],
                recv_sem=hr.at[sweep, way, i],
                device_id=at_slab(z),
                device_id_type=MESH,
            )
            for way, (src, plane, z) in enumerate(
                ((tail, HALO - 1 - i, up), (head, HALO + PLANES + i, down))
            )
        ]

    def class_copies(i):
        return [
            pltpu.make_async_remote_copy(
                src_ref=cm_in.at[src],
                dst_ref=cm.at[plane],
                send_sem=cs.at[way, i],
                recv_sem=cr.at[way, i],
                device_id=at_slab(z),
                device_id_type=MESH,
            )
            for way, (src, plane, z) in enumerate(
                ((PLANES - 1 - i, HALO - 1 - i, up), (i, HALO + PLANES + i, down))
            )
        ]

    for i in range(HALO):
        for copy in halo_copies(0, i):
            copy.start()
        if i < HALO - 1:
            for copy in class_copies(i):
                copy.start()

    def diffusivity(plane):
        klass = cm[plane]
        for field in range(2):
            value = jnp.zeros(klass.shape, jnp.float32)
            for k in range(CLASSES):
                value = jnp.where(klass == k, table[k, field], value)
            lam[plane, field] = value

    for copy in loads:
        copy.wait()

    def own_lam(p, carry):
        diffusivity(HALO + p)
        return carry

    lax.fori_loop(0, PLANES, own_lam, 0)

    def fine(base, level, plane):
        u, v = lv[base + level - 1, plane, 0], lv[base + level - 1, plane, 1]
        lap_u = lv[base + level - 1, plane - 1, 0] + lv[base + level - 1, plane + 1, 0]
        lap_v = lv[base + level - 1, plane - 1, 1] + lv[base + level - 1, plane + 1, 1]
        lap_u = lap_u + four(u) - 6.0 * u
        lap_v = lap_v + four(v) - 6.0 * v
        ru, rv = react(u, v, STEP)
        return u + lam[plane, 0] * lap_u + ru, v + lam[plane, 1] * lap_v + rv

    def fine_group(base, d):
        def step(k, carry):
            low = HALO - d + k
            for plane in (low, DEEP - 1 - low):
                u, v = fine(base, k, plane)
                lv[base + k, plane, 0] = u
                lv[base + k, plane, 1] = v
            return carry

        lax.fori_loop(1, min(d + 1, FINE - 1) + 1, step, 0)

    def guesses(sweep):
        keep = jnp.where(t == sweep, 0.0, 1.0).astype(jnp.float32)

        def one(p, carry):
            q = HALO + p
            cu, cv = coarse_of(lam[q, 0]), coarse_of(lam[q, 1])
            gu, gv = coarse(lv[4 * sweep, q, 0], lv[4 * sweep, q, 1], cu, cv)
            gb[p, 0] = keep * gu
            gb[p, 1] = keep * gv
            return carry

        lax.fori_loop(0, PLANES, one, 0)

    def piece_copy(sweep, owner):
        return pltpu.make_async_remote_copy(
            src_ref=pack.at[sweep, owner],
            dst_ref=got.at[sweep, t],
            send_sem=ps.at[sweep, owner],
            recv_sem=pr.at[sweep, t],
            device_id=(owner, s),
            device_id_type=MESH,
        )

    lane = lax.broadcasted_iota(jnp.int32, (8, LANES), 1)

    def last_step(sweep, q):
        p = q - HALO
        u, v = fine(4 * sweep, FINE, q)
        @pl.when(t == sweep)
        def _():
            out[0, 0, p] = u
            out[0, 1, p] = v
        u = u - gb[p, 0]
        v = v - gb[p, 1]
        for c in range(CHUNKS):
            owner = p * CHUNKS + c
            here = slice(c * LANES, (c + 1) * LANES)
            after = ((c + 1) % CHUNKS) * LANES
            before = ((c - 1) % CHUNKS) * LANES
            pack[sweep, owner, 0:ROWS] = u[:, here]
            pack[sweep, owner, ROWS : 2 * ROWS] = v[:, here]
            edges = None
            for quarter, (field, row) in enumerate(((u, 0), (u, 8), (v, 0), (v, 8))):
                both = jnp.where(
                    lane < 64,
                    field[row : row + 8, after : after + LANES],
                    field[row : row + 8, before : before + LANES],
                )
                both = pltpu.roll(both, 32 * quarter + 16, 1)
                edges = both if edges is None else jnp.where(lane // 32 == quarter, both, edges)
            pack[sweep, owner, 2 * ROWS : PIECE] = edges

        def send(c, carry):
            owner = p * CHUNKS + c

            @pl.when(owner != t)
            def _():
                piece_copy(sweep, owner).start()

            @pl.when(owner == t)
            def _():
                pltpu.make_async_copy(
                    pack.at[sweep, owner], got.at[sweep, t], pr.at[sweep, t]
                ).start()

            return carry

        lax.fori_loop(0, CHUNKS, send, 0)

    def propagate(sweep):
        base = 4 * sweep
        fine_group(base, 0)
        guesses(sweep)
        for d in range(1, HALO + 1):
            for copy in halo_copies(sweep, d - 1):
                copy.wait_recv()
            if sweep == 0 and d >= 2:
                for copy in class_copies(d - 2):
                    copy.wait_recv()
                diffusivity(HALO + 1 - d)
                diffusivity(HALO + PLANES - 2 + d)
            fine_group(base, d)
            if d + 1 >= FINE:
                low = 2 * HALO - d
                last_step(sweep, low)
                last_step(sweep, DEEP - 1 - low)

    def state_copy(sweep, target, src):
        columns = pl.ds(pl.multiple_of(my_chunk * LANES, LANES), LANES)
        if sweep == 0:
            dst = lv.at[4, HALO + my_plane, :, :, columns]
        else:
            dst = out.at[0, :, my_plane, :, columns]
        return (
            pltpu.make_async_remote_copy(
                src_ref=src,
                dst_ref=dst,
                send_sem=vs.at[sweep, target],
                recv_sem=vr.at[sweep, my_plane],
                device_id=(target, s),
                device_id_type=MESH,
            ),
            pltpu.make_async_copy(src, dst, vr.at[sweep, my_plane]),
        )

    def send_state(sweep, target, src):
        remote, local = state_copy(sweep, target, src)

        @pl.when(target != t)
        def _():
            remote.start()

        @pl.when(target == t)
        def _():
            local.start()

    def wait_piece(sweep, j):
        pltpu.make_async_copy(got.at[sweep, j], got.at[sweep, j], pr.at[sweep, j]).wait()

    def unpack(sweep, j):
        edges = got[sweep, j, 2 * ROWS : PIECE]
        parts = [pltpu.roll(edges, LANES - (32 * quarter + 16), 1) for quarter in range(4)]
        fields = []
        for field in range(2):
            side = jnp.concatenate(parts[2 * field : 2 * field + 2], axis=0)
            main = got[sweep, j, field * ROWS : (field + 1) * ROWS]
            fields.append(jnp.concatenate([main, side], axis=1))
        return fields

    def relay(sweep):
        columns = [
            pl.ds(pl.multiple_of(lax.rem(my_chunk + k, CHUNKS) * LANES, LANES), LANES)
            for k in (0, 1, CHUNKS - 1)
        ]
        wide = lax.broadcasted_iota(jnp.int32, (ROWS, LANES), 1)
        maps = []
        for field in range(2):
            here, after, before = [lam[HALO + my_plane, field, :, c] for c in columns]
            both = jnp.concatenate([here, jnp.where(wide < 64, after, before)], axis=1)
            maps.append(coarse_of(both))
        wait_piece(sweep, sweep)
        u, v = unpack(sweep, sweep)
        if sweep == 0:
            made[0, 0, 0] = u[:, :LANES]
            made[0, 0, 1] = v[:, :LANES]
            send_state(0, 1, made.at[0, 0])

        def step(m, carry):
            u, v = carry
            j = m + sweep
            wait_piece(sweep, j)
            cu, cv = unpack(sweep, j)
            u, v = coarse(u, v, maps[0], maps[1])
            u, v = u + cu, v + cv
            made[sweep, m, 0] = u[:, :LANES]
            made[sweep, m, 1] = v[:, :LANES]
            send_state(sweep, m + 1, made.at[sweep, m])
            return u, v

        lax.fori_loop(1, NTS - 1, step, (u, v))

    @pl.when(t < NTS - 1)
    def _():
        propagate(0)

    @pl.when(t == NTS - 1)
    def _():
        for d in range(HALO):
            for copy in halo_copies(0, d):
                copy.wait_recv()
            if d < HALO - 1:
                for copy in class_copies(d):
                    copy.wait_recv()
                diffusivity(HALO - 1 - d)
                diffusivity(HALO + PLANES + d)

    relay(0)

    def wait_plane(sweep, p):
        if sweep == 0:
            ref = lv.at[4, HALO + p]
        else:
            ref = out.at[0, :, p]
        pltpu.make_async_copy(ref, ref, vr.at[sweep, p]).wait()

    @pl.when(t > 0)
    def _():
        for i in range(HALO):
            if i < 2:
                wait_plane(0, PLANES - 1 - i)
                wait_plane(0, i)
            for copy in halo_copies(1, i):
                copy.start()
        propagate(1)

    relay(1)

    @pl.when(t > 1)
    def _():
        for p in range(PLANES):
            wait_plane(1, p)

    for i in range(HALO):
        for copy in halo_copies(0, i):
            copy.wait_send()
        if i < HALO - 1:
            for copy in class_copies(i):
                copy.wait_send()

    @pl.when(t > 0)
    def _():
        for i in range(HALO):
            for copy in halo_copies(1, i):
                copy.wait_send()

    for sweep in range(2):
        sender = t < NTS - 1 if sweep == 0 else t > 0

        def drain(owner, carry):
            @pl.when(sender & (owner != t))
            def _():
                piece_copy(sweep, owner).wait_send()

            @pl.when((owner != t) & (owner > sweep))
            def _():
                state_copy(sweep, owner, made.at[sweep, 0])[0].wait_send()

            return carry

        lax.fori_loop(0, NTS, drain, 0)


def on_device(slice_starts, class_map, table):
    field = (2, ROWS, COLS)
    return pl.pallas_call(
        kernel,
        out_shape=jax.ShapeDtypeStruct(slice_starts.shape, jnp.float32),
        in_specs=[
            pl.BlockSpec(memory_space=pl.ANY),
            pl.BlockSpec(memory_space=pl.ANY),
            pl.BlockSpec(memory_space=pltpu.SMEM),
        ],
        out_specs=pl.BlockSpec(memory_space=pltpu.VMEM),
        scratch_shapes=[
            pltpu.VMEM((2 * FINE, DEEP) + field, jnp.float32),
            pltpu.VMEM((DEEP, ROWS, COLS), jnp.int32),
            pltpu.VMEM((DEEP,) + field, jnp.float32),
            pltpu.VMEM((PLANES,) + field, jnp.float32),
            pltpu.VMEM((2, NTS, PIECE, LANES), jnp.float32),
            pltpu.VMEM((2, NTS, PIECE, LANES), jnp.float32),
            pltpu.VMEM((2, NTS, 2, ROWS, LANES), jnp.float32),
            pltpu.SemaphoreType.DMA((PLANES + 1,)),
            pltpu.SemaphoreType.DMA((2, 2, HALO)),
            pltpu.SemaphoreType.DMA((2, 2, HALO)),
            pltpu.SemaphoreType.DMA((2, HALO - 1)),
            pltpu.SemaphoreType.DMA((2, HALO - 1)),
            pltpu.SemaphoreType.DMA((2, NTS)),
            pltpu.SemaphoreType.DMA((2, NTS)),
            pltpu.SemaphoreType.DMA((2, NTS)),
            pltpu.SemaphoreType.DMA((2, PLANES)),
        ],
        compiler_params=pltpu.CompilerParams(
            collective_id=0, has_side_effects=True, vmem_limit_bytes=32 * 1024 * 1024
        ),
        name="parareal",
    )(slice_starts, class_map, table)


def solution(mesh):
    in_specs = (P("tm", None, "slab", None, None), P("slab", None, None), P())
    out_specs = P("tm", None, "slab", None, None)
    return jax.shard_map(
        on_device, mesh=mesh, in_specs=in_specs, out_specs=out_specs, check_vma=False
    )
```

time: 404 us -> 74.6 us (0.18); the launches traced: 397 us -> 74.4 us
  waiting for transfers between devices: 232 us -> 0 us
  starting transfers between devices: 132 us -> 0 us
  Pallas kernels: 0 us -> 71.1 us
  other arithmetic: 17.3 us -> 0 us
  local copies, waits for them, and re-layouts: 14 us -> 3.32 us
    ppermute x46 -> x0, waiting for transfers between devices: 232 us -> none  [the longest x30 184 us: from_behind(): return lax.ppermute(block, axis, route)]
    ppermute x46 -> x0, starting transfers between devices: 132 us -> none  [the longest x30 78.4 us: from_behind(): return lax.ppermute(block, axis, route)]
    pallas_call x0 -> x1, Pallas kernels: none -> 71.1 us  [on_device(): pl.pallas_call(kernel, out_shape=jax.ShapeDtypeStruct(slice_starts.shape,...]
    add x75 -> x0, other arithmetic: 14.2 us -> none  [the longest x30 10.6 us: relay(): result = coarse_prop(current, coarse_lam) + corr]
    slice x165 -> x0, local copies, waits for them, and re-layouts: 12.4 us -> none  [the longest x74 7.93 us: inplane(): jnp.roll(field, -1, -1)]
  transfers between devices with their start and end apart: 46 -> 0, of which waited for: 38 -> 0; matrix products, arithmetic and copies ran while one was open for 0% -> 0% of each run, Pallas kernels for 0% -> 0%
where the time goes in v1:
time: 74.6 us; the launch traced here: 74.4 us
  Pallas kernels  71.1 us (95%)
  local copies, waits for them, and re-layouts  3.32 us (4%)
    pallas_call x1, Pallas kernels, on_device(): pl.pallas_call(kernel, out_shape=jax.ShapeDtypeStruct(slice_starts.shape,...  71.1 us
    unnamed x6, local copies, waits for them, and re-layouts  3.32 us

profile of v1, /device:TPU:7, one launch (start us, length us, event | category | flops | bytes accessed | tf_op | source)
XLA Modules:
  0.0 74.4 jit_solution(13342560597251352543)
XLA Ops:
  0.0 0.8 %copy.4.table = f32[4,2]{1,0:T(4,128)S(1)} copy(f32[4,2]{0,1:T(2,128)} %param.5) | data formatting | bytes 64 | tf_op args[2]
  0.8 0.0 copy-start
  0.8 0.9 %copy-done = f32[1,2,4,16,512]{4,3,2,1,0:T(8,128)S(1)} copy-done((f32[1,2,4,16,512]{4,3,2,1,0:T(8,128)S(1)}, f32[1,2,4,16,512]{4,3,2,1,0:T(8,128)}, u32[]{:S(2)}) %copy-start) | copy-done | bytes 262168
  1.7 0.0 copy-start.1
  1.7 0.9 %copy-done.1 = s32[4,16,512]{2,1,0:T(8,128)S(1)} copy-done((s32[4,16,512]{2,1,0:T(8,128)S(1)}, s32[4,16,512]{2,1,0:T(8,128)}, u32[]{:S(2)}) %copy-start.1) | copy-done | bytes 131096
  2.6 71.1 %parareal.1 = f32[1,2,4,16,512]{4,3,2,1,0:T(8,128)S(1)} custom-call(f32[1,2,4,16,512]{4,3,2,1,0:T(8,128)S(1)} %copy-done, s32[4,16,512]{2,1,0:T(8,128)S(1)} %copy-done.1, f32[4,2]{1,0:T(4,128)S(1)} %copy.4.table), custom_call_target="tpu_custom_call" | custom-call | tf_op jit(solution)/shard_map/parareal/pallas_call | solution.py:399
  73.7 0.7 copy.6
Async XLA Ops:
  0.8 0.9 %copy-start = (f32[1,2,4,16,512]{4,3,2,1,0:T(8,128)S(1)}, f32[1,2,4,16,512]{4,3,2,1,0:T(8,128)}, u32[]{:S(2)}) copy-start(f32[1,2,4,16,512]{4,3,2,1,0:T(8,128)} %ss.1) | copy-start | bytes 786436
  1.7 0.9 %copy-start.1 = (s32[4,16,512]{2,1,0:T(8,128)S(1)}, s32[4,16,512]{2,1,0:T(8,128)}, u32[]{:S(2)}) copy-start(s32[4,16,512]{2,1,0:T(8,128)} %cm_in.1) | copy-start | bytes 393220

commit v2 on v1

--- a/solution.py
+++ b/solution.py
@@ -22,6 +22,8 @@
 DEEP = PLANES + 2 * HALO
 PIECE = 2 * ROWS + 8
 MESH = pl.DeviceIdType.MESH
+TALL = 8
+ROUND = ((3, 0), (3, 1), (2, 1))
 
 
 def react(u, v, scale):
@@ -50,8 +52,9 @@
 
 def kernel(
     ss, cm_in, table, out,
-    lv, cm, lam, gb, pack, got, made,
-    load_sem, hs, hr, cs, cr, ps, pr, vs, vr,
+    lv, cm, lam, gb, pack, got, made, tails, heads, kinds, planes,
+    load_sem, hs, hr, ts, tr, ds, dr, cs, cr, xs, xr, ks, kr,
+    gs, gr, es, er, fs, ps, pr, vs, vr, ready, here,
 ):
     t = lax.axis_index("tm")
     s = lax.axis_index("slab")
@@ -60,20 +63,50 @@
     down = lax.rem(s + slabs - 1, slabs)
     my_plane = t // CHUNKS
     my_chunk = lax.rem(t, CHUNKS)
-
-    def at_slab(z):
-        return (t, z)
+    my_columns = pl.ds(pl.multiple_of(my_chunk * LANES, LANES), LANES)
+    core = lax.rem(t, 2)
+    partner = t + 1 - 2 * core
+    last = t == NTS - 1
+    height = lax.rem(s, TALL)
+    top, bottom = height == TALL - 1, height == 0
+    end = top | bottom
+    across = jnp.where(top, s - (TALL - 1), jnp.where(bottom, s + (TALL - 1), s))
+    beside_up = lax.rem(s + TALL, slabs)
+    beside_down = lax.rem(s + slabs - TALL, slabs)
+    UP, DOWN = 0, 1
+
+    def signal(sem, where):
+        pl.semaphore_signal(sem, inc=1, device_id=where, device_id_type=MESH)
+
+    def remote(src, dst, send, recv, where):
+        return pltpu.make_async_remote_copy(
+            src_ref=src,
+            dst_ref=dst,
+            send_sem=send,
+            recv_sem=recv,
+            device_id=where,
+            device_id_type=MESH,
+        )
+
+    def arrived(ref, sem):
+        pltpu.make_async_copy(ref, ref, sem).wait()
 
     barrier = pltpu.get_barrier_semaphore()
-    for z in (up, down):
-        pl.semaphore_signal(barrier, inc=1, device_id=at_slab(z), device_id_type=MESH)
-
-    def greet(k, carry):
-        peer = lax.rem(t + k, NTS)
-        pl.semaphore_signal(barrier, inc=1, device_id=(peer, s), device_id_type=MESH)
-        return carry
-
-    lax.fori_loop(1, NTS, greet, 0)
+    signal(barrier, (partner, s))
+    signal(barrier, (t, down))
+
+    @pl.when(jnp.logical_not(top))
+    def _():
+        signal(barrier, (t, up))
+
+    @pl.when(bottom)
+    def _():
+        for z in (across, beside_up, beside_down):
+            signal(barrier, (t, z))
+
+    @pl.when(jnp.logical_not(last | end))
+    def _():
+        signal(barrier, (NTS - 1, s))
 
     loads = [
         pltpu.make_async_copy(ss.at[0, :, p], lv.at[0, HALO + p], load_sem.at[p])
@@ -82,55 +115,305 @@
     loads.append(pltpu.make_async_copy(cm_in, cm.at[pl.ds(HALO, PLANES)], load_sem.at[PLANES]))
     for copy in loads:
         copy.start()
-    pl.semaphore_wait(barrier, NTS + 1)
-
-    def halo_copies(sweep, i):
-        if sweep == 0:
-            tail, head = ss.at[0, :, PLANES - 1 - i], ss.at[0, :, i]
-        else:
-            tail, head = lv.at[4, HALO + PLANES - 1 - i], lv.at[4, HALO + i]
-        return [
-            pltpu.make_async_remote_copy(
-                src_ref=src,
-                dst_ref=lv.at[4 * sweep, plane],
-                send_sem=hs.at[sweep, way, i],
-                recv_sem=hr.at[sweep, way, i],
-                device_id=at_slab(z),
-                device_id_type=MESH,
-            )
-            for way, (src, plane, z) in enumerate(
-                ((tail, HALO - 1 - i, up), (head, HALO + PLANES + i, down))
-            )
-        ]
-
-    def class_copies(i):
-        return [
-            pltpu.make_async_remote_copy(
-                src_ref=cm_in.at[src],
-                dst_ref=cm.at[plane],
-                send_sem=cs.at[way, i],
-                recv_sem=cr.at[way, i],
-                device_id=at_slab(z),
-                device_id_type=MESH,
-            )
-            for way, (src, plane, z) in enumerate(
-                ((PLANES - 1 - i, HALO - 1 - i, up), (i, HALO + PLANES + i, down))
-            )
-        ]
-
-    for i in range(HALO):
-        for copy in halo_copies(0, i):
+    pl.semaphore_wait(barrier, 3 + jnp.where(end, 1, 0) + jnp.where(last, NTS - 1, 0))
+
+    @pl.when(top)
+    def _():
+        signal(here, (t, up))
+        signal(here, (t, across))
+
+        @pl.when(jnp.logical_not(last))
+        def _():
+            signal(barrier, (NTS - 1, s))
+
+    @pl.when(last)
+    def _():
+        @pl.when(bottom)
+        def _():
+            pl.semaphore_wait(here, 2)
+
+        def tell(peer, carry):
+            signal(ready, (peer, s))
+            return carry
+
+        lax.fori_loop(0, NTS - 1, tell, 0)
+
+    def carrier(way):
+        return ((core == way) & (t < NTS - 2)) | (t == NTS - 2)
+
+    def class_planes(way, i):
+        return (PLANES - 1 - i, HALO - 1 - i) if way == UP else (i, HALO + PLANES + i)
+
+    def class_copy(way, i):
+        src, plane = class_planes(way, i)
+        return remote(
+            cm_in.at[src], cm.at[plane], cs.at[way, i], cr.at[way, i], (t, down if way else up)
+        )
+
+    def kind_copy(i):
+        return remote(cm_in.at[i], kinds.at[i], cs.at[DOWN, i], kr.at[i], (t, beside_down))
+
+    def kind_forward(i):
+        return remote(
+            kinds.at[i], cm.at[HALO + PLANES + i], ks.at[i], cr.at[DOWN, i], (t, across)
+        )
+
+    def class_share(way, i):
+        plane = class_planes(way, i)[1]
+        return remote(cm.at[plane], cm.at[plane], xs.at[way, i], xr.at[way, i], (partner, s))
+
+    def send_class():
+        @pl.when(carrier(UP))
+        def _():
+            for i in range(HALO - 1):
+                class_copy(UP, i).start()
+
+        @pl.when(carrier(DOWN) & bottom)
+        def _():
+            for i in range(HALO - 1):
+                kind_copy(i).start()
+
+        @pl.when(carrier(DOWN) & jnp.logical_not(bottom))
+        def _():
+            for i in range(HALO - 1):
+                class_copy(DOWN, i).start()
+
+    def pass_class():
+        @pl.when(carrier(DOWN))
+        def _():
+            for i in range(HALO - 1):
+                copy = kind_forward(i)
+                kind_copy(i).wait_recv()
+                copy.start()
+
+    def share_class():
+        for way in (UP, DOWN):
+
+            @pl.when(carrier(way))
+            def _():
+                for i in range(HALO - 1):
+                    share = class_share(way, i)
+                    class_copy(way, i).wait_recv()
+                    share.start()
+
+    def take_class(i):
+        for way in (UP, DOWN):
+
+            @pl.when(jnp.logical_not(carrier(way)))
+            def _():
+                class_share(way, i).wait_recv()
+
+        diffusivity(HALO - 1 - i)
+        diffusivity(HALO + PLANES + i)
+
+    def drain_class():
+        for way in (UP, DOWN):
+
+            @pl.when(carrier(way))
+            def _():
+                for i in range(HALO - 1):
+                    class_copy(way, i).wait_send()
+                    class_share(way, i).wait_send()
+
+        @pl.when(bottom & carrier(DOWN))
+        def _():
+            for i in range(HALO - 1):
+                kind_forward(i).wait_send()
+
+    def unit_source(way, i, field):
+        return ss.at[0, field, PLANES - 1 - i if way == UP else i]
+
+    def unit_target(way, i, field):
+        return lv.at[0, HALO - 1 - i if way == UP else HALO + PLANES + i, field]
+
+    def unit_copy(way, i, field):
+        return remote(
+            unit_source(way, i, field),
+            unit_target(way, i, field),
+            hs.at[way, i, field],
+            hr.at[way, i, field],
+            (t, up if way == UP else down),
+        )
+
+    def tail_copy(n):
+        i, field = ROUND[n]
+        return remote(
+            unit_source(UP, i, field), tails.at[n], hs.at[UP, i, field], tr.at[n], (t, across)
+        )
+
+    def tail_forward(n):
+        i, field = ROUND[n]
+        return remote(
+            tails.at[n], unit_target(UP, i, field), ts.at[n], hr.at[UP, i, field], (t, beside_up)
+        )
+
+    def head_copy(i, field):
+        return remote(
+            unit_source(DOWN, i, field),
+            heads.at[i, field],
+            hs.at[DOWN, i, field],
+            dr.at[i, field],
+            (t, beside_down),
+        )
+
+    def head_forward(i, field):
+        return remote(
+            heads.at[i, field],
+            unit_target(DOWN, i, field),
+            ds.at[i, field],
+            hr.at[DOWN, i, field],
+            (t, across),
+        )
+
+    UNITS = [(i, field) for i in range(HALO) for field in range(2)]
+
+    def send_starts():
+        @pl.when(top)
+        def _():
+            for i, field in UNITS[:2]:
+                unit_copy(UP, i, field).start()
+            for n in range(len(ROUND)):
+                tail_copy(n).start()
+            for i, field in UNITS[2:]:
+                if (i, field) not in ROUND:
+                    unit_copy(UP, i, field).start()
+            for i, field in UNITS:
+                unit_copy(DOWN, i, field).start()
+
+        @pl.when(bottom)
+        def _():
+            for i, field in UNITS:
+                head_copy(i, field).start()
+                unit_copy(UP, i, field).start()
+
+        @pl.when(jnp.logical_not(end))
+        def _():
+            for i, field in UNITS:
+                unit_copy(UP, i, field).start()
+                unit_copy(DOWN, i, field).start()
+
+    def pass_heads(units):
+        for i, field in units:
+            copy = head_forward(i, field)
+            head_copy(i, field).wait_recv()
             copy.start()
-        if i < HALO - 1:
-            for copy in class_copies(i):
+
+    def pass_tails():
+        for n in range(len(ROUND)):
+            copy = tail_forward(n)
+            tail_copy(n).wait_recv()
+            copy.start()
+
+    def drain_starts():
+        for way in (UP, DOWN):
+            for i, field in UNITS:
+                unit_copy(way, i, field).wait_send()
+
+        @pl.when(bottom)
+        def _():
+            for i, field in UNITS:
+                head_forward(i, field).wait_send()
+            for n in range(len(ROUND)):
+                tail_forward(n).wait_send()
+
+    def outer(way, i):
+        return lv.at[4, HALO - 1 - i if way == UP else HALO + PLANES + i]
+
+    def plane_copy(way, i):
+        return remote(
+            lv.at[4, HALO + (PLANES - 1 - i if way == UP else i)],
+            outer(way, i),
+            gs.at[way, i],
+            gr.at[way, i],
+            (t, up if way == UP else down),
+        )
+
+    def send_planes(each):
+        for way, over in ((UP, top), (DOWN, bottom)):
+
+            @pl.when(jnp.logical_not(over))
+            def _():
+                for i in each:
+                    plane_copy(way, i).start()
+
+    def plane_forward(i):
+        n = i - HALO // 2
+        return remote(
+            planes.at[n],
+            lv.at[4, jnp.where(bottom, HALO - 1 - i, HALO + PLANES + i)],
+            fs.at[n],
+            gr.at[jnp.where(bottom, UP, DOWN), i],
+            (t, jnp.where(bottom, beside_up, beside_down)),
+        )
+
+    def pass_planes():
+        @pl.when(end)
+        def _():
+            for i in range(HALO // 2, HALO):
+                n = i - HALO // 2
+                copy = plane_forward(i)
+                arrived(planes.at[n], er.at[n])
                 copy.start()
+
+    def drain_planes():
+        for way, over in ((UP, top), (DOWN, bottom)):
+
+            @pl.when(jnp.logical_not(over))
+            def _():
+                for i in range(HALO):
+                    plane_copy(way, i).wait_send()
+
+        @pl.when(end)
+        def _():
+            for i in range(HALO // 2, HALO):
+                plane_forward(i).wait_send()
+
+    far = jnp.where(top, PLANES - 1 - my_plane, my_plane)
+
+    def straight_copy(target, src):
+        return remote(
+            src,
+            lv.at[4, jnp.where(top, my_plane, HALO + PLANES + my_plane), :, :, my_columns],
+            es.at[target],
+            gr.at[jnp.where(top, UP, DOWN), far],
+            (target, jnp.where(top, up, down)),
+        )
+
+    def round_copy(target, src):
+        n = jnp.where(far < HALO // 2, 0, far - HALO // 2)
+        return remote(
+            src, planes.at[n, :, :, my_columns], es.at[target], er.at[n], (target, across)
+        )
+
+    def send_over(target, src):
+        @pl.when(end & (far < HALO // 2))
+        def _():
+            straight_copy(target, src).start()
+
+        @pl.when(end & (far >= HALO // 2))
+        def _():
+            round_copy(target, src).start()
+
+    def wait_halo(sweep, i):
+        for way in (UP, DOWN):
+            if sweep == 0:
+                for field in range(2):
+                    unit_copy(way, i, field).wait_recv()
+            else:
+                arrived(outer(way, i), gr.at[way, i])
+
+    send_class()
+
+    @pl.when(jnp.logical_not(last))
+    def _():
+        send_starts()
 
     def diffusivity(plane):
         klass = cm[plane]
         for field in range(2):
             value = jnp.zeros(klass.shape, jnp.float32)
             for k in range(CLASSES):
-                value = jnp.where(klass == k, table[k, field], value)
+                value = jnp.where(klass == k, table[field, k], value)
             lam[plane, field] = value
 
     for copy in loads:
@@ -235,26 +518,36 @@
         base = 4 * sweep
         fine_group(base, 0)
         guesses(sweep)
+        if sweep == 0:
+            @pl.when(bottom)
+            def _():
+                pl.semaphore_wait(here, 2)
+                signal(barrier, (NTS - 1, s))
+                pass_class()
+                pass_heads(UNITS[:2])
+                pass_tails()
+                pass_heads(UNITS[2:])
+
+            share_class()
+        else:
+            pass_planes()
         for d in range(1, HALO + 1):
-            for copy in halo_copies(sweep, d - 1):
-                copy.wait_recv()
+            wait_halo(sweep, d - 1)
             if sweep == 0 and d >= 2:
-                for copy in class_copies(d - 2):
-                    copy.wait_recv()
-                diffusivity(HALO + 1 - d)
-                diffusivity(HALO + PLANES - 2 + d)
+                take_class(d - 2)
             fine_group(base, d)
             if d + 1 >= FINE:
+                if sweep == 0 and d + 1 == FINE:
+                    pl.semaphore_wait(ready, 1)
                 low = 2 * HALO - d
                 last_step(sweep, low)
                 last_step(sweep, DEEP - 1 - low)
 
     def state_copy(sweep, target, src):
-        columns = pl.ds(pl.multiple_of(my_chunk * LANES, LANES), LANES)
         if sweep == 0:
-            dst = lv.at[4, HALO + my_plane, :, :, columns]
+            dst = lv.at[4, HALO + my_plane, :, :, my_columns]
         else:
-            dst = out.at[0, :, my_plane, :, columns]
+            dst = out.at[0, :, my_plane, :, my_columns]
         return (
             pltpu.make_async_remote_copy(
                 src_ref=src,
@@ -268,15 +561,18 @@
         )
 
     def send_state(sweep, target, src):
-        remote, local = state_copy(sweep, target, src)
+        there, local = state_copy(sweep, target, src)
 
         @pl.when(target != t)
         def _():
-            remote.start()
+            there.start()
 
         @pl.when(target == t)
         def _():
             local.start()
+
+        if sweep == 0:
+            send_over(target, src)
 
     def wait_piece(sweep, j):
         pltpu.make_async_copy(got.at[sweep, j], got.at[sweep, j], pr.at[sweep, j]).wait()
@@ -323,20 +619,14 @@
 
         lax.fori_loop(1, NTS - 1, step, (u, v))
 
-    @pl.when(t < NTS - 1)
+    @pl.when(jnp.logical_not(last))
     def _():
         propagate(0)
 
-    @pl.when(t == NTS - 1)
-    def _():
-        for d in range(HALO):
-            for copy in halo_copies(0, d):
-                copy.wait_recv()
-            if d < HALO - 1:
-                for copy in class_copies(d):
-                    copy.wait_recv()
-                diffusivity(HALO - 1 - d)
-                diffusivity(HALO + PLANES + d)
+    @pl.when(last)
+    def _():
+        for i in range(HALO - 1):
+            take_class(i)
 
     relay(0)
 
@@ -349,12 +639,12 @@
 
     @pl.when(t > 0)
     def _():
-        for i in range(HALO):
-            if i < 2:
-                wait_plane(0, PLANES - 1 - i)
-                wait_plane(0, i)
-            for copy in halo_copies(1, i):
-                copy.start()
+        wait_plane(0, PLANES - 1)
+        wait_plane(0, 0)
+        send_planes((0, 3))
+        wait_plane(0, 1)
+        wait_plane(0, 2)
+        send_planes((1, 2))
         propagate(1)
 
     relay(1)
@@ -364,18 +654,15 @@
         for p in range(PLANES):
             wait_plane(1, p)
 
-    for i in range(HALO):
-        for copy in halo_copies(0, i):
-            copy.wait_send()
-        if i < HALO - 1:
-            for copy in class_copies(i):
-                copy.wait_send()
+    drain_class()
+
+    @pl.when(jnp.logical_not(last))
+    def _():
+        drain_starts()
 
     @pl.when(t > 0)
     def _():
-        for i in range(HALO):
-            for copy in halo_copies(1, i):
-                copy.wait_send()
+        drain_planes()
 
     for sweep in range(2):
         sender = t < NTS - 1 if sweep == 0 else t > 0
@@ -389,13 +676,18 @@
             def _():
                 state_copy(sweep, owner, made.at[sweep, 0])[0].wait_send()
 
+            if sweep == 0:
+                @pl.when(end & (owner > 0))
+                def _():
+                    straight_copy(owner, made.at[0, 0]).wait_send()
+
             return carry
 
         lax.fori_loop(0, NTS, drain, 0)
 
 
 def on_device(slice_starts, class_map, table):
-    field = (2, ROWS, COLS)
+    field, dma = (2, ROWS, COLS), pltpu.SemaphoreType.DMA
     return pl.pallas_call(
         kernel,
         out_shape=jax.ShapeDtypeStruct(slice_starts.shape, jnp.float32),
@@ -413,21 +705,40 @@
             pltpu.VMEM((2, NTS, PIECE, LANES), jnp.float32),
             pltpu.VMEM((2, NTS, PIECE, LANES), jnp.float32),
             pltpu.VMEM((2, NTS, 2, ROWS, LANES), jnp.float32),
-            pltpu.SemaphoreType.DMA((PLANES + 1,)),
-            pltpu.SemaphoreType.DMA((2, 2, HALO)),
-            pltpu.SemaphoreType.DMA((2, 2, HALO)),
-            pltpu.SemaphoreType.DMA((2, HALO - 1)),
-            pltpu.SemaphoreType.DMA((2, HALO - 1)),
-            pltpu.SemaphoreType.DMA((2, NTS)),
-            pltpu.SemaphoreType.DMA((2, NTS)),
-            pltpu.SemaphoreType.DMA((2, NTS)),
-            pltpu.SemaphoreType.DMA((2, PLANES)),
+            pltpu.VMEM((len(ROUND), ROWS, COLS), jnp.float32),
+            pltpu.VMEM((HALO, 2, ROWS, COLS), jnp.float32),
+            pltpu.VMEM((HALO - 1, ROWS, COLS), jnp.int32),
+            pltpu.VMEM((HALO // 2,) + field, jnp.float32),
+            dma((PLANES + 1,)),
+            dma((2, HALO, 2)),
+            dma((2, HALO, 2)),
+            dma((len(ROUND),)),
+            dma((len(ROUND),)),
+            dma((HALO, 2)),
+            dma((HALO, 2)),
+            dma((2, HALO - 1)),
+            dma((2, HALO - 1)),
+            dma((2, HALO - 1)),
+            dma((2, HALO - 1)),
+            dma((HALO - 1,)),
+            dma((HALO - 1,)),
+            dma((2, HALO)),
+            dma((2, HALO)),
+            dma((NTS,)),
+            dma((HALO // 2,)),
+            dma((HALO // 2,)),
+            dma((2, NTS)),
+            dma((2, NTS)),
+            dma((2, NTS)),
+            dma((2, PLANES)),
+            pltpu.SemaphoreType.REGULAR,
+            pltpu.SemaphoreType.REGULAR,
         ],
         compiler_params=pltpu.CompilerParams(
-            collective_id=0, has_side_effects=True, vmem_limit_bytes=32 * 1024 * 1024
+            collective_id=0, has_side_effects=True, vmem_limit_bytes=60 * 1024 * 1024
         ),
         name="parareal",
-    )(slice_starts, class_map, table)
+    )(slice_starts, class_map, table.T)
 
 
 def solution(mesh):

time: 74.6 us -> 65.1 us (0.87)
  Pallas kernels: 71.1 us -> 63.2 us
  local copies, waits for them, and re-layouts: 3.32 us -> 1.67 us
    pallas_call x1, Pallas kernels: 71.1 us -> 63.2 us  [on_device(): pl.pallas_call(kernel, out_shape=jax.ShapeDtypeStruct(slice_starts.shape,...]
    unnamed x6 -> x1, local copies, waits for them, and re-layouts: 3.32 us -> 1.67 us
where the time goes in v2:
time: 65.1 us; the launch traced here: 64.9 us
  Pallas kernels  63.2 us (97%)
  local copies, waits for them, and re-layouts  1.67 us (3%)
    pallas_call x1, Pallas kernels, on_device(): pl.pallas_call(kernel, out_shape=jax.ShapeDtypeStruct(slice_starts.shape,...  63.2 us
    unnamed x1, local copies, waits for them, and re-layouts  1.67 us

profile of v2, /device:TPU:7, one launch (start us, length us, event | category | flops | bytes accessed | tf_op | source)
XLA Modules:
  0.0 64.9 jit_solution(8898099126850759781)
XLA Ops:
  0.0 63.2 %parareal.1 = f32[1,2,4,16,512]{4,3,2,1,0:T(8,128)} custom-call(f32[1,2,4,16,512]{4,3,2,1,0:T(8,128)} %ss.1, s32[4,16,512]{2,1,0:T(8,128)} %cm_in.1, f32[2,4]{1,0:T(2,128)} %bitcast.1), custom_call_target="tpu_custom_call" | custom-call | tf_op jit(solution)/shard_map/parareal/pallas_call | solution.py:691
  63.2 1.7 %copy.5 = f32[1,2,4,16,512]{4,3,2,1,0:T(8,128)} copy(f32[1,2,4,16,512]{4,3,2,1,0:T(8,128)} %parareal.1) | data formatting | bytes 524288

commit v3 on v2

--- a/solution.py
+++ b/solution.py
@@ -24,6 +24,7 @@
 MESH = pl.DeviceIdType.MESH
 TALL = 8
 ROUND = ((3, 0), (3, 1), (2, 1))
+NEAR = 2
 
 
 def react(u, v, scale):
@@ -61,8 +62,8 @@
     slabs = lax.axis_size("slab")
     up = lax.rem(s + 1, slabs)
     down = lax.rem(s + slabs - 1, slabs)
-    my_plane = t // CHUNKS
-    my_chunk = lax.rem(t, CHUNKS)
+    my_plane = lax.rem(t, PLANES)
+    my_chunk = t // PLANES
     my_columns = pl.ds(pl.multiple_of(my_chunk * LANES, LANES), LANES)
     core = lax.rem(t, 2)
     partner = t + 1 - 2 * core
@@ -337,7 +338,7 @@
                     plane_copy(way, i).start()
 
     def plane_forward(i):
-        n = i - HALO // 2
+        n = i - NEAR
         return remote(
             planes.at[n],
             lv.at[4, jnp.where(bottom, HALO - 1 - i, HALO + PLANES + i)],
@@ -349,8 +350,8 @@
     def pass_planes():
         @pl.when(end)
         def _():
-            for i in range(HALO // 2, HALO):
-                n = i - HALO // 2
+            for i in range(NEAR, HALO):
+                n = i - NEAR
                 copy = plane_forward(i)
                 arrived(planes.at[n], er.at[n])
                 copy.start()
@@ -365,7 +366,7 @@
 
         @pl.when(end)
         def _():
-            for i in range(HALO // 2, HALO):
+            for i in range(NEAR, HALO):
                 plane_forward(i).wait_send()
 
     far = jnp.where(top, PLANES - 1 - my_plane, my_plane)
@@ -380,17 +381,17 @@
         )
 
     def round_copy(target, src):
-        n = jnp.where(far < HALO // 2, 0, far - HALO // 2)
+        n = jnp.where(far < NEAR, 0, far - NEAR)
         return remote(
             src, planes.at[n, :, :, my_columns], es.at[target], er.at[n], (target, across)
         )
 
     def send_over(target, src):
-        @pl.when(end & (far < HALO // 2))
+        @pl.when(end & (far < NEAR))
         def _():
             straight_copy(target, src).start()
 
-        @pl.when(end & (far >= HALO // 2))
+        @pl.when(end & (far >= NEAR))
         def _():
             round_copy(target, src).start()
 
@@ -480,7 +481,7 @@
         u = u - gb[p, 0]
         v = v - gb[p, 1]
         for c in range(CHUNKS):
-            owner = p * CHUNKS + c
+            owner = c * PLANES + p
             here = slice(c * LANES, (c + 1) * LANES)
             after = ((c + 1) % CHUNKS) * LANES
             before = ((c - 1) % CHUNKS) * LANES
@@ -498,7 +499,7 @@
             pack[sweep, owner, 2 * ROWS : PIECE] = edges
 
         def send(c, carry):
-            owner = p * CHUNKS + c
+            owner = c * PLANES + p
 
             @pl.when(owner != t)
             def _():
@@ -571,8 +572,6 @@
         def _():
             local.start()
 
-        if sweep == 0:
-            send_over(target, src)
 
     def wait_piece(sweep, j):
         pltpu.make_async_copy(got.at[sweep, j], got.at[sweep, j], pr.at[sweep, j]).wait()
@@ -618,6 +617,12 @@
             return u, v
 
         lax.fori_loop(1, NTS - 1, step, (u, v))
+        if sweep == 0:
+            def over(k, carry):
+                send_over(k + 1, made.at[0, k])
+                return carry
+
+            lax.fori_loop(0, NTS - 1, over, 0)
 
     @pl.when(jnp.logical_not(last))
     def _():
@@ -690,7 +695,7 @@
     field, dma = (2, ROWS, COLS), pltpu.SemaphoreType.DMA
     return pl.pallas_call(
         kernel,
-        out_shape=jax.ShapeDtypeStruct(slice_starts.shape, jnp.float32),
+        out_shape=pltpu.VMEM(slice_starts.shape, jnp.float32),
         in_specs=[
             pl.BlockSpec(memory_space=pl.ANY),
             pl.BlockSpec(memory_space=pl.ANY),
@@ -708,7 +713,7 @@
             pltpu.VMEM((len(ROUND), ROWS, COLS), jnp.float32),
             pltpu.VMEM((HALO, 2, ROWS, COLS), jnp.float32),
             pltpu.VMEM((HALO - 1, ROWS, COLS), jnp.int32),
-            pltpu.VMEM((HALO // 2,) + field, jnp.float32),
+            pltpu.VMEM((HALO - NEAR,) + field, jnp.float32),
             dma((PLANES + 1,)),
             dma((2, HALO, 2)),
             dma((2, HALO, 2)),
@@ -725,8 +730,8 @@
             dma((2, HALO)),
             dma((2, HALO)),
             dma((NTS,)),
-            dma((HALO // 2,)),
-            dma((HALO // 2,)),
+            dma((HALO - NEAR,)),
+            dma((HALO - NEAR,)),
             dma((2, NTS)),
             dma((2, NTS)),
             dma((2, NTS)),

time: 65.1 us -> 59.8 us (0.919)
  Pallas kernels: 63.2 us -> 58.5 us
  local copies, waits for them, and re-layouts: 1.67 us -> 0.71 us
    pallas_call x1, Pallas kernels: 63.2 us -> 58.5 us  [on_device(): pl.pallas_call(kernel, out_shape=pltpu.VMEM(slice_starts.shape, jnp.float...]
    unnamed x1, local copies, waits for them, and re-layouts: 1.67 us -> 0.71 us
where the time goes in v3:
time: 59.8 us; the launch traced here: 59.3 us
  Pallas kernels  58.5 us (98%)
  local copies, waits for them, and re-layouts  0.71 us (1%)
    pallas_call x1, Pallas kernels, on_device(): pl.pallas_call(kernel, out_shape=pltpu.VMEM(slice_starts.shape, jnp.float...  58.5 us

profile of v3, /device:TPU:7, one launch (start us, length us, event | category | flops | bytes accessed | tf_op | source)
XLA Modules:
  0.0 59.3 jit_solution(18436201582487658223)
XLA Ops:
  0.0 58.5 %parareal.1 = f32[1,2,4,16,512]{4,3,2,1,0:T(8,128)S(1)} custom-call(f32[1,2,4,16,512]{4,3,2,1,0:T(8,128)} %ss.1, s32[4,16,512]{2,1,0:T(8,128)} %cm_in.1, f32[2,4]{1,0:T(2,128)} %bitcast.1), custom_call_target="tpu_custom_call" | custom-call | tf_op jit(solution)/shard_map/parareal/pallas_call | solution.py:696
  58.5 0.7 %copy.5 = f32[1,2,4,16,512]{4,3,2,1,0:T(8,128)} copy(f32[1,2,4,16,512]{4,3,2,1,0:T(8,128)S(1)} %parareal.1) | data formatting | bytes 524288

commit v4 on v3

--- a/solution.py
+++ b/solution.py
@@ -25,6 +25,7 @@
 TALL = 8
 ROUND = ((3, 0), (3, 1), (2, 1))
 NEAR = 2
+LATE = ((3, 0), (3, 1))
 
 
 def react(u, v, scale):
@@ -53,8 +54,8 @@
 
 def kernel(
     ss, cm_in, table, out,
-    lv, cm, lam, gb, pack, got, made, tails, heads, kinds, planes,
-    load_sem, hs, hr, ts, tr, ds, dr, cs, cr, xs, xr, ks, kr,
+    lv, cm, lam, gb, pack, got, made, tails, heads, late, kinds, planes,
+    load_sem, hs, hr, ts, tr, ls, lr, ds, dr, cs, cr, xs, xr, ks, kr,
     gs, gr, es, er, fs, ps, pr, vs, vr, ready, here,
 ):
     t = lax.axis_index("tm")
@@ -148,20 +149,20 @@
     def class_copy(way, i):
         src, plane = class_planes(way, i)
         return remote(
-            cm_in.at[src], cm.at[plane], cs.at[way, i], cr.at[way, i], (t, down if way else up)
+            cm_in.at[src], cm.at[plane], cs.at[way], cr.at[way, i], (t, down if way else up)
         )
 
     def kind_copy(i):
-        return remote(cm_in.at[i], kinds.at[i], cs.at[DOWN, i], kr.at[i], (t, beside_down))
+        return remote(cm_in.at[i], kinds.at[i], cs.at[DOWN], kr.at[i], (t, beside_down))
 
     def kind_forward(i):
         return remote(
-            kinds.at[i], cm.at[HALO + PLANES + i], ks.at[i], cr.at[DOWN, i], (t, across)
+            kinds.at[i], cm.at[HALO + PLANES + i], ks, cr.at[DOWN, i], (t, across)
         )
 
     def class_share(way, i):
         plane = class_planes(way, i)[1]
-        return remote(cm.at[plane], cm.at[plane], xs.at[way, i], xr.at[way, i], (partner, s))
+        return remote(cm.at[plane], cm.at[plane], xs.at[way], xr.at[way, i], (partner, s))
 
     def send_class():
         @pl.when(carrier(UP))
@@ -208,18 +209,17 @@
         diffusivity(HALO + PLANES + i)
 
     def drain_class():
+        some = cm.at[pl.ds(0, HALO - 1)]
         for way in (UP, DOWN):
 
             @pl.when(carrier(way))
             def _():
-                for i in range(HALO - 1):
-                    class_copy(way, i).wait_send()
-                    class_share(way, i).wait_send()
+                arrived(some, cs.at[way])
+                arrived(some, xs.at[way])
 
         @pl.when(bottom & carrier(DOWN))
         def _():
-            for i in range(HALO - 1):
-                kind_forward(i).wait_send()
+            arrived(kinds, ks)
 
     def unit_source(way, i, field):
         return ss.at[0, field, PLANES - 1 - i if way == UP else i]
@@ -231,7 +231,7 @@
         return remote(
             unit_source(way, i, field),
             unit_target(way, i, field),
-            hs.at[way, i, field],
+            hs.at[way],
             hr.at[way, i, field],
             (t, up if way == UP else down),
         )
@@ -239,20 +239,20 @@
     def tail_copy(n):
         i, field = ROUND[n]
         return remote(
-            unit_source(UP, i, field), tails.at[n], hs.at[UP, i, field], tr.at[n], (t, across)
+            unit_source(UP, i, field), tails.at[n], hs.at[UP], tr.at[n], (t, across)
         )
 
     def tail_forward(n):
         i, field = ROUND[n]
         return remote(
-            tails.at[n], unit_target(UP, i, field), ts.at[n], hr.at[UP, i, field], (t, beside_up)
+            tails.at[n], unit_target(UP, i, field), ts, hr.at[UP, i, field], (t, beside_up)
         )
 
     def head_copy(i, field):
         return remote(
             unit_source(DOWN, i, field),
             heads.at[i, field],
-            hs.at[DOWN, i, field],
+            hs.at[DOWN],
             dr.at[i, field],
             (t, beside_down),
         )
@@ -261,12 +261,29 @@
         return remote(
             heads.at[i, field],
             unit_target(DOWN, i, field),
-            ds.at[i, field],
+            ds,
             hr.at[DOWN, i, field],
             (t, across),
         )
 
+    def late_copy(n):
+        i, field = LATE[n]
+        return remote(
+            unit_source(DOWN, i, field), late.at[n], hs.at[DOWN], lr.at[n], (t, across)
+        )
+
+    def late_forward(n):
+        i, field = LATE[n]
+        return remote(
+            late.at[n],
+            unit_target(DOWN, i, field),
+            ls,
+            hr.at[DOWN, i, field],
+            (t, beside_down),
+        )
+
     UNITS = [(i, field) for i in range(HALO) for field in range(2)]
+    EARLY = [unit for unit in UNITS if unit not in LATE]
 
     def send_starts():
         @pl.when(top)
@@ -284,7 +301,8 @@
         @pl.when(bottom)
         def _():
             for i, field in UNITS:
-                head_copy(i, field).start()
+                if (i, field) in EARLY:
+                    head_copy(i, field).start()
                 unit_copy(UP, i, field).start()
 
         @pl.when(jnp.logical_not(end))
@@ -305,17 +323,24 @@
             tail_copy(n).wait_recv()
             copy.start()
 
+    def pass_late():
+        for n in range(len(LATE)):
+            copy = late_forward(n)
+            late_copy(n).wait_recv()
+            copy.start()
+
     def drain_starts():
         for way in (UP, DOWN):
-            for i, field in UNITS:
-                unit_copy(way, i, field).wait_send()
+            arrived(lv.at[0, pl.ds(0, HALO)], hs.at[way])
 
         @pl.when(bottom)
         def _():
-            for i, field in UNITS:
-                head_forward(i, field).wait_send()
-            for n in range(len(ROUND)):
-                tail_forward(n).wait_send()
+            arrived(heads.at[pl.ds(0, len(EARLY) // 2)], ds)
+            arrived(tails, ts)
+
+        @pl.when(top)
+        def _():
+            arrived(late, ls)
 
     def outer(way, i):
         return lv.at[4, HALO - 1 - i if way == UP else HALO + PLANES + i]
@@ -324,7 +349,7 @@
         return remote(
             lv.at[4, HALO + (PLANES - 1 - i if way == UP else i)],
             outer(way, i),
-            gs.at[way, i],
+            gs.at[way],
             gr.at[way, i],
             (t, up if way == UP else down),
         )
@@ -342,7 +367,7 @@
         return remote(
             planes.at[n],
             lv.at[4, jnp.where(bottom, HALO - 1 - i, HALO + PLANES + i)],
-            fs.at[n],
+            fs,
             gr.at[jnp.where(bottom, UP, DOWN), i],
             (t, jnp.where(bottom, beside_up, beside_down)),
         )
@@ -361,13 +386,11 @@
 
             @pl.when(jnp.logical_not(over))
             def _():
-                for i in range(HALO):
-                    plane_copy(way, i).wait_send()
+                arrived(lv.at[4, pl.ds(0, HALO)], gs.at[way])
 
         @pl.when(end)
         def _():
-            for i in range(NEAR, HALO):
-                plane_forward(i).wait_send()
+            arrived(planes, fs)
 
     far = jnp.where(top, PLANES - 1 - my_plane, my_plane)
 
@@ -375,7 +398,7 @@
         return remote(
             src,
             lv.at[4, jnp.where(top, my_plane, HALO + PLANES + my_plane), :, :, my_columns],
-            es.at[target],
+            es,
             gr.at[jnp.where(top, UP, DOWN), far],
             (target, jnp.where(top, up, down)),
         )
@@ -383,7 +406,7 @@
     def round_copy(target, src):
         n = jnp.where(far < NEAR, 0, far - NEAR)
         return remote(
-            src, planes.at[n, :, :, my_columns], es.at[target], er.at[n], (target, across)
+            src, planes.at[n, :, :, my_columns], es, er.at[n], (target, across)
         )
 
     def send_over(target, src):
@@ -463,7 +486,7 @@
         return pltpu.make_async_remote_copy(
             src_ref=pack.at[sweep, owner],
             dst_ref=got.at[sweep, t],
-            send_sem=ps.at[sweep, owner],
+            send_sem=ps.at[sweep],
             recv_sem=pr.at[sweep, t],
             device_id=(owner, s),
             device_id_type=MESH,
@@ -498,8 +521,8 @@
                 edges = both if edges is None else jnp.where(lane // 32 == quarter, both, edges)
             pack[sweep, owner, 2 * ROWS : PIECE] = edges
 
-        def send(c, carry):
-            owner = c * PLANES + p
+        def send(k, carry):
+            owner = lax.rem(my_chunk + CHUNKS + 2 - k, CHUNKS) * PLANES + p
 
             @pl.when(owner != t)
             def _():
@@ -517,6 +540,8 @@
 
     def propagate(sweep):
         base = 4 * sweep
+        if sweep == 1:
+            pass_planes()
         fine_group(base, 0)
         guesses(sweep)
         if sweep == 0:
@@ -524,14 +549,21 @@
             def _():
                 pl.semaphore_wait(here, 2)
                 signal(barrier, (NTS - 1, s))
+                for n in range(len(LATE)):
+                    late_copy(n).start()
                 pass_class()
-                pass_heads(UNITS[:2])
+                pass_heads(EARLY[:2])
                 pass_tails()
-                pass_heads(UNITS[2:])
+                pass_heads(EARLY[2:])
 
             share_class()
-        else:
-            pass_planes()
+
+            @pl.when(top)
+            def _():
+                pass_late()
+
+        if sweep == 1:
+            drain_first()
         for d in range(1, HALO + 1):
             wait_halo(sweep, d - 1)
             if sweep == 0 and d >= 2:
@@ -553,7 +585,7 @@
             pltpu.make_async_remote_copy(
                 src_ref=src,
                 dst_ref=dst,
-                send_sem=vs.at[sweep, target],
+                send_sem=vs.at[sweep],
                 recv_sem=vr.at[sweep, my_plane],
                 device_id=(target, s),
                 device_id_type=MESH,
@@ -572,6 +604,26 @@
         def _():
             local.start()
 
+
+    def drain_pieces(sweep):
+        arrived(pack.at[sweep, pl.ds(0, NTS - 1)], ps.at[sweep])
+
+    def drain_states(sweep):
+        for own in (0, 1):
+
+            @pl.when((t > sweep) == bool(own))
+            def _():
+                arrived(made.at[sweep, pl.ds(0, NTS - 1 - sweep - own)], vs.at[sweep])
+
+    def drain_first():
+        drain_class()
+
+        @pl.when(jnp.logical_not(last))
+        def _():
+            drain_starts()
+            drain_pieces(0)
+
+        drain_states(0)
 
     def wait_piece(sweep, j):
         pltpu.make_async_copy(got.at[sweep, j], got.at[sweep, j], pr.at[sweep, j]).wait()
@@ -652,43 +704,27 @@
         send_planes((1, 2))
         propagate(1)
 
+    @pl.when(t == 0)
+    def _():
+        drain_first()
+
+    @pl.when(end)
+    def _():
+        arrived(made.at[0, pl.ds(0, NTS - 1)], es)
+
     relay(1)
+
+    @pl.when(t > 0)
+    def _():
+        drain_planes()
+        drain_pieces(1)
 
     @pl.when(t > 1)
     def _():
         for p in range(PLANES):
             wait_plane(1, p)
 
-    drain_class()
-
-    @pl.when(jnp.logical_not(last))
-    def _():
-        drain_starts()
-
-    @pl.when(t > 0)
-    def _():
-        drain_planes()
-
-    for sweep in range(2):
-        sender = t < NTS - 1 if sweep == 0 else t > 0
-
-        def drain(owner, carry):
-            @pl.when(sender & (owner != t))
-            def _():
-                piece_copy(sweep, owner).wait_send()
-
-            @pl.when((owner != t) & (owner > sweep))
-            def _():
-                state_copy(sweep, owner, made.at[sweep, 0])[0].wait_send()
-
-            if sweep == 0:
-                @pl.when(end & (owner > 0))
-                def _():
-                    straight_copy(owner, made.at[0, 0]).wait_send()
-
-            return carry
-
-        lax.fori_loop(0, NTS, drain, 0)
+    drain_states(1)
 
 
 def on_device(slice_starts, class_map, table):
@@ -712,29 +748,32 @@
             pltpu.VMEM((2, NTS, 2, ROWS, LANES), jnp.float32),
             pltpu.VMEM((len(ROUND), ROWS, COLS), jnp.float32),
             pltpu.VMEM((HALO, 2, ROWS, COLS), jnp.float32),
+            pltpu.VMEM((len(LATE), ROWS, COLS), jnp.float32),
             pltpu.VMEM((HALO - 1, ROWS, COLS), jnp.int32),
             pltpu.VMEM((HALO - NEAR,) + field, jnp.float32),
             dma((PLANES + 1,)),
+            dma((2,)),
             dma((2, HALO, 2)),
-            dma((2, HALO, 2)),
+            dma,
             dma((len(ROUND),)),
-            dma((len(ROUND),)),
+            dma,
+            dma((len(LATE),)),
+            dma,
             dma((HALO, 2)),
-            dma((HALO, 2)),
+            dma((2,)),
             dma((2, HALO - 1)),
+            dma((2,)),
             dma((2, HALO - 1)),
-            dma((2, HALO - 1)),
-            dma((2, HALO - 1)),
+            dma,
             dma((HALO - 1,)),
-            dma((HALO - 1,)),
+            dma((2,)),
             dma((2, HALO)),
-            dma((2, HALO)),
-            dma((NTS,)),
+            dma,
             dma((HALO - NEAR,)),
-            dma((HALO - NEAR,)),
+            dma,
+            dma((2,)),
             dma((2, NTS)),
-            dma((2, NTS)),
-            dma((2, NTS)),
+            dma((2,)),
             dma((2, PLANES)),
             pltpu.SemaphoreType.REGULAR,
             pltpu.SemaphoreType.REGULAR,

time: 59.8 us -> 57.5 us (0.962)
  Pallas kernels: 58.5 us -> 56.4 us
    pallas_call x1, Pallas kernels: 58.5 us -> 56.4 us  [on_device(): pl.pallas_call(kernel, out_shape=pltpu.VMEM(slice_starts.shape, jnp.float...]
where the time goes in v4:
time: 57.5 us; the launch traced here: 57.1 us
  Pallas kernels  56.4 us (98%)
  local copies, waits for them, and re-layouts  0.71 us (1%)
    pallas_call x1, Pallas kernels, on_device(): pl.pallas_call(kernel, out_shape=pltpu.VMEM(slice_starts.shape, jnp.float...  56.4 us

profile of v4, /device:TPU:7, one launch (start us, length us, event | category | flops | bytes accessed | tf_op | source)
XLA Modules:
  0.0 57.1 jit_solution(12246511177382247381)
XLA Ops:
  0.0 56.4 %parareal.1 = f32[1,2,4,16,512]{4,3,2,1,0:T(8,128)S(1)} custom-call(f32[1,2,4,16,512]{4,3,2,1,0:T(8,128)} %ss.1, s32[4,16,512]{2,1,0:T(8,128)} %cm_in.1, f32[2,4]{1,0:T(2,128)} %bitcast.1), custom_call_target="tpu_custom_call" | custom-call | tf_op jit(solution)/shard_map/parareal/pallas_call | solution.py:732
  56.4 0.7 %copy.5 = f32[1,2,4,16,512]{4,3,2,1,0:T(8,128)} copy(f32[1,2,4,16,512]{4,3,2,1,0:T(8,128)S(1)} %parareal.1) | data formatting | bytes 524288

commit v5 on v4

--- a/solution.py
+++ b/solution.py
@@ -285,14 +285,14 @@
     UNITS = [(i, field) for i in range(HALO) for field in range(2)]
     EARLY = [unit for unit in UNITS if unit not in LATE]
 
+    def send_tails():
+        for n in range(len(ROUND)):
+            tail_copy(n).start()
+
     def send_starts():
         @pl.when(top)
         def _():
-            for i, field in UNITS[:2]:
-                unit_copy(UP, i, field).start()
-            for n in range(len(ROUND)):
-                tail_copy(n).start()
-            for i, field in UNITS[2:]:
+            for i, field in UNITS:
                 if (i, field) not in ROUND:
                     unit_copy(UP, i, field).start()
             for i, field in UNITS:
@@ -409,22 +409,28 @@
             src, planes.at[n, :, :, my_columns], es, er.at[n], (target, across)
         )
 
-    def send_over(target, src):
-        @pl.when(end & (far < NEAR))
-        def _():
-            straight_copy(target, src).start()
-
-        @pl.when(end & (far >= NEAR))
-        def _():
-            round_copy(target, src).start()
-
-    def wait_halo(sweep, i):
-        for way in (UP, DOWN):
-            if sweep == 0:
-                for field in range(2):
-                    unit_copy(way, i, field).wait_recv()
-            else:
-                arrived(outer(way, i), gr.at[way, i])
+    def send_over(where):
+        for there, copy in ((far < NEAR, straight_copy), (far >= NEAR, round_copy)):
+
+            @pl.when(where & there)
+            def _():
+                def one(k, carry):
+                    copy(k + 1, made.at[0, k]).start()
+                    return carry
+
+                lax.fori_loop(0, NTS - 1, one, 0)
+
+    def wait_side(sweep, i, side):
+        plane = jnp.where(side == UP, HALO - 1 - i, HALO + PLANES + i)
+        if sweep == 0:
+            for field in range(2):
+                arrived(lv.at[0, plane, field], hr.at[side, i, field])
+        else:
+            arrived(lv.at[4, plane], gr.at[side, i])
+
+    @pl.when(top & jnp.logical_not(last))
+    def _():
+        send_tails()
 
     send_class()
 
@@ -458,16 +464,22 @@
         ru, rv = react(u, v, STEP)
         return u + lam[plane, 0] * lap_u + ru, v + lam[plane, 1] * lap_v + rv
 
-    def fine_group(base, d):
+    def fine_side(base, d, side):
         def step(k, carry):
             low = HALO - d + k
-            for plane in (low, DEEP - 1 - low):
-                u, v = fine(base, k, plane)
-                lv[base + k, plane, 0] = u
-                lv[base + k, plane, 1] = v
+            plane = jnp.where(side == UP, low, DEEP - 1 - low)
+            u, v = fine(base, k, plane)
+            lv[base + k, plane, 0] = u
+            lv[base + k, plane, 1] = v
             return carry
 
         lax.fori_loop(1, min(d + 1, FINE - 1) + 1, step, 0)
+
+    def fine_inside(base):
+        for plane in (HALO + 1, HALO + 2):
+            u, v = fine(base, 1, plane)
+            lv[base + 1, plane, 0] = u
+            lv[base + 1, plane, 1] = v
 
     def guesses(sweep):
         keep = jnp.where(t == sweep, 0.0, 1.0).astype(jnp.float32)
@@ -542,7 +554,7 @@
         base = 4 * sweep
         if sweep == 1:
             pass_planes()
-        fine_group(base, 0)
+        fine_inside(base)
         guesses(sweep)
         if sweep == 0:
             @pl.when(bottom)
@@ -565,16 +577,17 @@
         if sweep == 1:
             drain_first()
         for d in range(1, HALO + 1):
-            wait_halo(sweep, d - 1)
             if sweep == 0 and d >= 2:
                 take_class(d - 2)
-            fine_group(base, d)
-            if d + 1 >= FINE:
-                if sweep == 0 and d + 1 == FINE:
-                    pl.semaphore_wait(ready, 1)
-                low = 2 * HALO - d
-                last_step(sweep, low)
-                last_step(sweep, DEEP - 1 - low)
+            for turn in range(2):
+                side = jnp.where(top, turn, 1 - turn)
+                wait_side(sweep, d - 1, side)
+                fine_side(base, d, side)
+                if d + 1 >= FINE:
+                    if sweep == 0 and d + 1 == FINE and turn == 0:
+                        pl.semaphore_wait(ready, 1)
+                    low = 2 * HALO - d
+                    last_step(sweep, jnp.where(side == UP, low, DEEP - 1 - low))
 
     def state_copy(sweep, target, src):
         if sweep == 0:
@@ -670,11 +683,7 @@
 
         lax.fori_loop(1, NTS - 1, step, (u, v))
         if sweep == 0:
-            def over(k, carry):
-                send_over(k + 1, made.at[0, k])
-                return carry
-
-            lax.fori_loop(0, NTS - 1, over, 0)
+            send_over(top)
 
     @pl.when(jnp.logical_not(last))
     def _():
@@ -696,16 +705,15 @@
 
     @pl.when(t > 0)
     def _():
-        wait_plane(0, PLANES - 1)
-        wait_plane(0, 0)
-        send_planes((0, 3))
-        wait_plane(0, 1)
-        wait_plane(0, 2)
-        send_planes((1, 2))
+        for p in range(PLANES):
+            wait_plane(0, p)
+        send_planes(range(HALO))
+        send_over(bottom)
         propagate(1)
 
     @pl.when(t == 0)
     def _():
+        send_over(bottom)
         drain_first()
 
     @pl.when(end)

time: 57.5 us -> 56.1 us (0.976)
  Pallas kernels: 56.4 us -> 54.9 us
    pallas_call x1, Pallas kernels: 56.4 us -> 54.9 us  [on_device(): pl.pallas_call(kernel, out_shape=pltpu.VMEM(slice_starts.shape, jnp.float...]
where the time goes in v5:
time: 56.1 us; the launch traced here: 55.6 us
  Pallas kernels  54.9 us (98%)
  local copies, waits for them, and re-layouts  0.71 us (1%)
    pallas_call x1, Pallas kernels, on_device(): pl.pallas_call(kernel, out_shape=pltpu.VMEM(slice_starts.shape, jnp.float...  54.9 us

profile of v5, /device:TPU:7, one launch (start us, length us, event | category | flops | bytes accessed | tf_op | source)
XLA Modules:
  0.0 55.6 jit_solution(1313824361023026605)
XLA Ops:
  0.0 54.9 %parareal.1 = f32[1,2,4,16,512]{4,3,2,1,0:T(8,128)S(1)} custom-call(f32[1,2,4,16,512]{4,3,2,1,0:T(8,128)} %ss.1, s32[4,16,512]{2,1,0:T(8,128)} %cm_in.1, f32[2,4]{1,0:T(2,128)} %bitcast.1), custom_call_target="tpu_custom_call" | custom-call | tf_op jit(solution)/shard_map/parareal/pallas_call | solution.py:740
  54.9 0.7 %copy.5 = f32[1,2,4,16,512]{4,3,2,1,0:T(8,128)} copy(f32[1,2,4,16,512]{4,3,2,1,0:T(8,128)S(1)} %parareal.1) | data formatting | bytes 524288

commit v6 on v5

--- a/solution.py
+++ b/solution.py
@@ -564,9 +564,9 @@
                 for n in range(len(LATE)):
                     late_copy(n).start()
                 pass_class()
-                pass_heads(EARLY[:2])
+                pass_heads(EARLY[:3])
                 pass_tails()
-                pass_heads(EARLY[2:])
+                pass_heads(EARLY[3:])
 
             share_class()
 

time: 56.1 us -> 55.8 us (level)
  no operation moved by 1% of the time
where the time goes in v6:
time: 55.8 us; the launch traced here: 55.4 us
  Pallas kernels  54.6 us (98%)
  local copies, waits for them, and re-layouts  0.71 us (1%)
    pallas_call x1, Pallas kernels, on_device(): pl.pallas_call(kernel, out_shape=pltpu.VMEM(slice_starts.shape, jnp.float...  54.6 us

profile of v6, /device:TPU:7, one launch (start us, length us, event | category | flops | bytes accessed | tf_op | source)
XLA Modules:
  0.0 55.4 jit_solution(7402008741770212013)
XLA Ops:
  0.0 54.6 %parareal.1 = f32[1,2,4,16,512]{4,3,2,1,0:T(8,128)S(1)} custom-call(f32[1,2,4,16,512]{4,3,2,1,0:T(8,128)} %ss.1, s32[4,16,512]{2,1,0:T(8,128)} %cm_in.1, f32[2,4]{1,0:T(2,128)} %bitcast.1), custom_call_target="tpu_custom_call" | custom-call | tf_op jit(solution)/shard_map/parareal/pallas_call | solution.py:740
  54.7 0.7 %copy.5 = f32[1,2,4,16,512]{4,3,2,1,0:T(8,128)} copy(f32[1,2,4,16,512]{4,3,2,1,0:T(8,128)S(1)} %parareal.1) | data formatting | bytes 524288
